TPU v7x, 256 devices: a whole 4x4x8 slice. The times are simulated.
256 devices in a mesh: wide: 64 (over z, x, core), narrow: 4 (over y).
Axes of the slice: x: 4, y: 4, z: 8, core: 2. Of those that a mesh axis runs over, the one named last changes fastest.
Arguments:
- snapshots: bfloat16 [524288, 512], P('wide', 'narrow'), may hold values from -16 to 16
Outputs:
- basis: float32 [524288, 128], P('wide', 'narrow')
- energies: float32 [128], P('narrow')
All inputs are finite; a program needn't handle non-finite values.
Results may differ from a plain program's by a relative error of at most 0.012.
Values may be sent and summed in bfloat16 or wider, within the bound.
A program may use at most 64 MiB of HBM per device.

v0:
```python
import jax
import jax.numpy as jnp
from jax import lax
from jax.sharding import PartitionSpec as P

ITERS = 3


epsilon = 1e-06


def shifted(value, axis, steps):
    count = lax.axis_size(axis)
    first, last = (max(0, -steps), min(count, count - steps))
    return lax.ppermute(value, axis, [(source, source + steps) for source in range(first, last)])


def spread(block, axis, holder):
    block = jnp.where(lax.axis_index(axis) == holder, block, jnp.zeros_like(block))
    return lax.psum(block, axis)


def orthonormal(tall):
    inner = jnp.dot(
        tall.T, tall, precision=lax.Precision.HIGHEST, preferred_element_type=jnp.float32
    )
    lower_factor = jnp.linalg.cholesky(inner)
    return lax.linalg.triangular_solve(
        lower_factor, tall, left_side=False, lower=True, transpose_a=True
    )


def rotation(gram_sum, basis_width):
    identity_block = jnp.eye(basis_width, dtype=jnp.float32)
    current = jnp.concatenate([identity_block, identity_block], axis=0) * jnp.float32(0.5**0.5)
    for sweep in range(ITERS):
        current = orthonormal(
            jnp.dot(
                gram_sum,
                current,
                precision=lax.Precision.HIGHEST,
                preferred_element_type=jnp.float32,
            )
        )
    return current.astype(jnp.bfloat16)


def body(snapshots):
    basis_width = snapshots.shape[1]
    tree_depth = lax.axis_size("narrow").bit_length() - 1
    position = lax.axis_index("narrow")
    current = snapshots
    gram_sum = None
    factor = None
    for tree_level in range(tree_depth):
        lower_part = current
        upper_part = shifted(current, "narrow", -(1 << tree_level))
        paired = jnp.concatenate([lower_part, upper_part], axis=1)
        local_gram = lax.dot_general(
            paired, paired, (((0,), (0,)), ((), ())), preferred_element_type=jnp.float32
        )
        gram_sum = lax.psum(local_gram, "wide")
        factor = rotation(gram_sum, basis_width)
        merged = jnp.dot(paired, factor, preferred_element_type=jnp.float32)
        if tree_level + 1 < tree_depth:
            current = merged.astype(jnp.bfloat16)
        else:
            current = merged
    squares = lax.psum(jnp.sum(current * current, axis=0), "wide")
    energies = jnp.sqrt(squares + epsilon)
    basis_out = current / energies
    basis_out, energies = (
        spread(basis_out.astype(jnp.bfloat16), "narrow", 0).astype(basis_out.dtype),
        spread(energies.astype(jnp.bfloat16), "narrow", 0).astype(energies.dtype),
    )
    own_width = basis_width // lax.axis_size("narrow")
    own_start = position * own_width
    basis_part = lax.dynamic_slice_in_dim(basis_out, own_start, own_width, 1)
    energy_part = lax.dynamic_slice_in_dim(energies, own_start, own_width, 0)
    return (basis_part, energy_part)


def solution(mesh):
    in_specs = (P("wide", "narrow"),)
    out_specs = (P("wide", "narrow"), P("narrow"))
    return jax.shard_map(body, mesh=mesh, in_specs=in_specs, out_specs=out_specs, check_vma=False)
```

profile of v0, /device:TPU:1, one launch (start us, length us, event | category | flops | bytes accessed | tf_op | source)
XLA Modules:
  0.0 828.1 jit_solution(169532295053082611)
XLA Ops:
  7.2 1.3 collective-permute-start
  8.5 2.0 constant_dynamic-update-slice_fusion.1
  10.5 44.1 %collective-permute-done = bf16[8192,128]{1,0:T(8,128)(2,1)S(1)} collective-permute-done((bf16[8192,128]{1,0:T(8,128)(2,1)}, bf16[8192,128]{1,0:T(8,128)(2,1)S(1)}, u32[]{:S(2)}, u32[]{:S(2)}) %collective-permute-start) | collective-permute-done | bytes 2097184 | tf_op jit(solution)/shard_map/ppermute | solution.py:15
  54.5 0.5 constant_dynamic-update-slice_fusion
  55.0 1.9 copy-done
  57.0 2.0 fusion.43
  59.2 181.3 %all-reduce.4.cloned.1.call-done = f32[256,256]{1,0:T(8,128)} async-done(((f32[256,256]{1,0:T(8,128)}), f32[256,256]{1,0:T(8,128)}) %all-reduce.4.cloned.1.call-update) | async-done | bytes 262160 | tf_op jit(solution)/shard_map/psum | solution.py:62
  240.6 1.3 fusion.7
  241.9 0.4 fusion.44
  242.4 11.7 %cholesky.104 = f32[128,128]{1,0:T(8,128)S(1)} custom-call(f32[128,128]{1,0:T(8,128)S(1)} %fusion.26), custom_call_target="Cholesky" | custom-call | tf_op jit(solution)/shard_map/jit(cholesky)/cholesky | solution.py:27
  254.1 0.6 compare_reduce_fusion.5
  254.8 0.7 fusion.9
  255.4 9.8 %custom-call.10 = f32[1,128,128]{1,2,0:T(8,128)S(1)} custom-call(f32[1,128,128]{2,1,0:T(8,128)S(1)} %fusion.9), custom_call_target="InvertDiagBlocksLowerTriangular" | custom-call | tf_op jit(solution)/shard_map/triangular_solve/custom-call.0 | solution.py:28
  265.3 0.3 convolution_bitcast_fusion.5
  265.6 1.3 fusion.45
  266.9 0.4 fusion.46
  267.4 11.7 %cholesky.115 = f32[128,128]{1,0:T(8,128)S(1)} custom-call(f32[128,128]{1,0:T(8,128)S(1)} %fusion.24), custom_call_target="Cholesky" | custom-call | tf_op jit(solution)/shard_map/jit(cholesky)/cholesky | solution.py:27
  279.2 0.6 compare_reduce_fusion.4
  279.8 0.7 fusion.10
  280.5 10.0 %custom-call.11 = f32[1,128,128]{1,2,0:T(8,128)S(1)} custom-call(f32[1,128,128]{2,1,0:T(8,128)S(1)} %fusion.10), custom_call_target="InvertDiagBlocksLowerTriangular" | custom-call | tf_op jit(solution)/shard_map/triangular_solve/custom-call.0 | solution.py:28
  290.5 0.3 convolution_bitcast_fusion.4
  290.8 1.3 fusion.47
  292.1 0.4 fusion.48
  292.6 11.7 %cholesky.126 = f32[128,128]{1,0:T(8,128)S(1)} custom-call(f32[128,128]{1,0:T(8,128)S(1)} %fusion.22), custom_call_target="Cholesky" | custom-call | tf_op jit(solution)/shard_map/jit(cholesky)/cholesky | solution.py:27
  304.4 0.6 compare_reduce_fusion.3
  305.0 0.7 fusion.11
  305.7 9.8 %custom-call.12 = f32[1,128,128]{1,2,0:T(8,128)S(1)} custom-call(f32[1,128,128]{2,1,0:T(8,128)S(1)} %fusion.11), custom_call_target="InvertDiagBlocksLowerTriangular" | custom-call | tf_op jit(solution)/shard_map/triangular_solve/custom-call.0 | solution.py:28
  315.5 0.3 fusion.3
  315.8 3.7 convolution_convert_fusion
  319.5 1.3 collective-permute-start.1
  320.8 49.1 %collective-permute-done.1 = bf16[8192,128]{0,1:T(8,128)(2,1)S(1)} collective-permute-done((bf16[8192,128]{0,1:T(8,128)(2,1)S(1)}, bf16[8192,128]{0,1:T(8,128)(2,1)S(1)}, u32[]{:S(2)}, u32[]{:S(2)}) %collective-permute-start.1) | collective-permute-done | bytes 2097184 | tf_op jit(solution)/shard_map/ppermute | solution.py:15
  369.9 1.3 copy-done.1
  371.2 2.0 fusion.1
  373.2 0.4 all-reduce.8.cloned.1.call-start
  373.7 169.9 %all-reduce.6.cloned.1.call-done = f32[256,256]{1,0:T(8,128)} async-done(((f32[256,256]{1,0:T(8,128)}), f32[256,256]{1,0:T(8,128)}) %all-reduce.6.cloned.1.call-update) | async-done | bytes 262160 | tf_op jit(solution)/shard_map/psum | solution.py:62
  543.6 1.3 fusion.5
  545.0 0.4 fusion.49
  545.5 11.7 %cholesky.137 = f32[128,128]{1,0:T(8,128)S(1)} custom-call(f32[128,128]{1,0:T(8,128)S(1)} %fusion.20), custom_call_target="Cholesky" | custom-call | tf_op jit(solution)/shard_map/jit(cholesky)/cholesky | solution.py:27
  557.2 0.6 compare_reduce_fusion.2
  557.9 0.7 fusion.12
  558.5 9.8 %custom-call.13 = f32[1,128,128]{1,2,0:T(8,128)S(1)} custom-call(f32[1,128,128]{2,1,0:T(8,128)S(1)} %fusion.12), custom_call_target="InvertDiagBlocksLowerTriangular" | custom-call | tf_op jit(solution)/shard_map/triangular_solve/custom-call.0 | solution.py:28
  568.3 0.3 convolution_bitcast_fusion.2
  568.7 1.3 fusion.50
  570.0 0.4 fusion.51
  570.5 11.7 %cholesky.148 = f32[128,128]{1,0:T(8,128)S(1)} custom-call(f32[128,128]{1,0:T(8,128)S(1)} %fusion.18), custom_call_target="Cholesky" | custom-call | tf_op jit(solution)/shard_map/jit(cholesky)/cholesky | solution.py:27
  582.3 0.6 compare_reduce_fusion.1
  582.9 0.7 fusion.13
  583.6 10.0 %custom-call.14 = f32[1,128,128]{1,2,0:T(8,128)S(1)} custom-call(f32[1,128,128]{2,1,0:T(8,128)S(1)} %fusion.13), custom_call_target="InvertDiagBlocksLowerTriangular" | custom-call | tf_op jit(solution)/shard_map/triangular_solve/custom-call.0 | solution.py:28
  593.5 0.3 convolution_bitcast_fusion.1
  593.8 1.3 fusion.52
  595.2 0.4 fusion.53
  595.7 11.7 %cholesky.159 = f32[128,128]{1,0:T(8,128)S(1)} custom-call(f32[128,128]{1,0:T(8,128)S(1)} %fusion.16), custom_call_target="Cholesky" | custom-call | tf_op jit(solution)/shard_map/jit(cholesky)/cholesky | solution.py:27
  607.4 0.6 compare_reduce_fusion
  608.1 0.7 fusion.14
  608.7 9.8 %custom-call.15 = f32[1,128,128]{1,2,0:T(8,128)S(1)} custom-call(f32[1,128,128]{2,1,0:T(8,128)S(1)} %fusion.14), custom_call_target="InvertDiagBlocksLowerTriangular" | custom-call | tf_op jit(solution)/shard_map/triangular_solve/custom-call.0 | solution.py:28
  618.6 0.3 fusion.4
  618.9 5.3 multiply_reduce_fusion
  624.1 122.6 %psum.37 = f32[128]{0:T(128)S(1)} all-reduce(f32[128]{0:T(128)S(1)} %get-tuple-element.6), channel_id=1, replica_groups=mesh['wide'=64,'narrow'=4] {'wide'}, use_global_device_ids=true, to_apply=%region_5.8 | all-reduce | flops 128 | bytes 1024 | tf_op jit(solution)/shard_map/psum | solution.py:69
  746.7 4.0 fusion.2
  750.7 8.5 %psum.39 = bf16[128]{0:T(256)(128)(2,1)S(1)} all-reduce(bf16[128]{0:T(256)(128)(2,1)S(1)} %broadcast_select_fusion), channel_id=1, replica_groups=mesh['wide'=64,'narrow'=4] {'narrow'}, use_global_device_ids=true, to_apply=%region_7.10 | all-reduce | flops 128 | bytes 512 | tf_op jit(solution)/shard_map/psum | solution.py:20
  759.2 0.6 dynamic_slice.7
  759.8 53.9 %all-reduce.8.cloned.1.call-done = bf16[8192,128]{1,0:T(8,128)(2,1)} async-done(((bf16[8192,128]{1,0:T(8,128)(2,1)}), bf16[8192,128]{1,0:T(8,128)(2,1)}) %all-reduce.8.cloned.1.call-update) | async-done | bytes 2097168 | tf_op jit(solution)/shard_map/psum | solution.py:20
  813.7 4.1 dynamic-slice_convert_fusion
  817.8 3.6 copy.9
  (28 shorter events, 1.2 us)
Async XLA Ops:
  7.2 233.4 %all-reduce.4.cloned.1.call-start = ((), (), s32[]{:S(2)}) async-start(), calls=%async_computation | async-start | bytes 524288 | tf_op jit(solution)/shard_map/psum | solution.py:62
  7.2 47.3 %collective-permute-start = (bf16[8192,128]{1,0:T(8,128)(2,1)}, bf16[8192,128]{1,0:T(8,128)(2,1)S(1)}, u32[]{:S(2)}, u32[]{:S(2)}) collective-permute-start(bf16[8192,128]{1,0:T(8,128)(2,1)} %param.4), channel_id=1, source_target_pairs={{1,0},{2,1},{3,2},{5,4},{6,5},{7,6},{9,8},{10,9},{11,10},{13,12},{... | collective-permute-start | bytes 6291464 | tf_op jit(solution)/shard_map/ppermute | solution.py:15
  55.0 1.9 copy-start
  59.0 484.7 %all-reduce.6.cloned.1.call-start = ((), (), s32[]{:S(2)}) async-start(), calls=%async_computation.1 | async-start | bytes 524288 | tf_op jit(solution)/shard_map/psum | solution.py:62
  319.5 50.4 %collective-permute-start.1 = (bf16[8192,128]{0,1:T(8,128)(2,1)S(1)}, bf16[8192,128]{0,1:T(8,128)(2,1)S(1)}, u32[]{:S(2)}, u32[]{:S(2)}) collective-permute-start(bf16[8192,128]{0,1:T(8,128)(2,1)S(1)} %convolution_convert_fusion), channel_id=1, source_target_pairs={{2,0},{3,1},{6,4},{7,5},{10,8},{11,9},{14,12},{15,13},{18,16},{19,... | collective-permute-start | bytes 6291464 | tf_op jit(solution)/shard_map/ppermute | solution.py:15
  369.9 1.3 copy-start.1
  373.2 440.4 %all-reduce.8.cloned.1.call-start = ((), (), s32[]{:S(2)}) async-start(), calls=%async_computation.2 | async-start | bytes 4194304 | tf_op jit(solution)/shard_map/psum | solution.py:20
Sparse Core Ops, SparseCore 0:
  59.1 181.4 all-reduce.3
  373.4 170.2 all-reduce.5
  750.8 62.7 all-reduce.7
where the time goes:
time: 831 us; the launch traced here: 828 us
  waiting for transfers between devices  498 us (60%)
  other arithmetic  146 us (18%)
  blocking collectives  131 us (16%)
  matrix products  25 us (3%)
  between operations  14.3 us (2%)
  local copies, waits for them, and re-layouts  10.4 us (1%)
    psum x2, waiting for transfers between devices, body(): gram_sum = lax.psum(local_gram, 'wide')  351 us
    psum x1, blocking collectives, body(): squares = lax.psum(jnp.sum(current * current, axis=0), 'wide')  123 us
    ppermute x2, waiting for transfers between devices, shifted(): lax.ppermute(value, axis, [(source, source + steps) for source in range(f...  93.2 us
    another operation x19, other arithmetic, orthonormal(): lower_factor = jnp.linalg.cholesky(inner)  74.3 us
    another operation x12, other arithmetic, orthonormal(): lax.linalg.triangular_solve(lower_factor, tall, left_side=False, lower=Tr...  63.1 us
    psum x1, waiting for transfers between devices, spread(): return lax.psum(block, axis)  53.9 us
  transfers between devices with their start and end apart: 5, of which 5 were waited for; matrix products, arithmetic and copies ran while one was open for 0% of the time, Pallas kernels for 0%

commit v1 on v0

v1 whole, which is shorter than its diff:
```python
import functools
import jax
import jax.numpy as jnp
from jax import lax
from jax.experimental import pallas as pl
from jax.experimental.pallas import tpu as pltpu
from jax.sharding import PartitionSpec as P

MESH = pl.DeviceIdType.MESH
F32 = jnp.float32
PAIRS = ((0, 0), (0, 1), (1, 1), (2, 2), (2, 3), (3, 3), (0, 2), (0, 3), (1, 2), (1, 3))
PARTS = ((0, 768), (768, 512))
VLIM = 48 * 1024 * 1024


def where_am_i():
    w = lax.axis_index("wide")
    y = lax.axis_index("narrow")
    return lax.rem(w, 2), lax.rem(lax.div(w, 2), 4), y, lax.div(w, 8)


def device(core, x, y, z):
    return {"wide": (z * 4 + x) * 2 + core, "narrow": y}


def greet(peers):
    barrier = pltpu.get_barrier_semaphore()
    for peer in peers:
        pl.semaphore_signal(barrier, inc=1, device_id=peer, device_id_type=MESH)
    pl.semaphore_wait(barrier, len(peers))


def remote(src, dst, send, recv, peer):
    return pltpu.make_async_remote_copy(src_ref=src, dst_ref=dst, send_sem=send, recv_sem=recv,
                                        device_id=peer, device_id_type=MESH)


def at(start, size, align=8):
    return pl.ds(pl.multiple_of(start, align), size)


def rows_kernel(s_ref, rows_ref, g_ref, stage_ref, send, recv, own_sem, *, gram=True, chunks=4, hw=False):
    core, x, y, z = where_am_i()
    R = rows_ref.shape[1]
    n = R // chunks
    up, down, far = (device(core, x, lax.rem(y + k, 4), z) for k in (1, 3, 2))
    to_up, to_down, to_far = lax.rem(y + 1, 4), lax.rem(y + 3, 4), lax.rem(y + 2, 4)
    greet([up, down, far])
    own = pltpu.make_async_copy(s_ref.at[at(y * R, R, 16)], rows_ref.at[y], own_sem)
    own.start()
    direct = [[], []]
    stage = [[], []]
    forward = [[], []]
    half = chunks // 2
    if not hw:
        for c in range(half):
            for side, peer in ((0, up), (1, down)):
                stage[side].append(remote(
                    s_ref.at[at(to_far * R + (side * half + c) * n, n, 16)], stage_ref.at[side, c],
                    send.at[side, c], recv.at[side, c], peer))
                stage[side][c].start()
    for c in range(chunks):
        for side, peer, row in ((0, up, to_up), (1, down, to_down)):
            direct[side].append(remote(
                s_ref.at[at(row * R + c * n, n, 16)], rows_ref.at[y, pl.ds(c * n, n)],
                send.at[side, half + c], recv.at[side, half + c], peer))
            direct[side][c].start()
    for c in range(half):
        for side, peer, origin in ((0, up, to_down), (1, down, to_up)):
            if hw:
                forward[side].append(remote(
                    s_ref.at[at(to_far * R + (side * half + c) * n, n, 16)],
                    rows_ref.at[y, pl.ds((side * half + c) * n, n)],
                    send.at[side, half + chunks + c], recv.at[side, half + chunks + c], far))
            else:
                stage[side][c].wait_recv()
                forward[side].append(remote(
                    stage_ref.at[side, c], rows_ref.at[origin, pl.ds((side * half + c) * n, n)],
                    send.at[side, half + chunks + c], recv.at[side, half + chunks + c], peer))
            forward[side][c].start()
    own.wait()
    if gram:
        g_ref[...] = jnp.zeros_like(g_ref)
    order = [c for pair in zip(range(half), range(half, chunks)) for c in pair]
    for c in order:
        direct[0][c].wait_recv()
        direct[1][c].wait_recv()
        forward[c // half][c % half].wait_recv()
        if gram:
            blocks = [rows_ref[j, pl.ds(c * n, n), :] for j in range(4)]
            for i in range(4):
                right = jnp.concatenate(blocks[i:], axis=1)
                part = lax.dot_general(blocks[i], right, (((0,), (0,)), ((), ())), preferred_element_type=F32)
                for j in range(i, 4):
                    b = PAIRS.index((i, j))
                    g_ref[128 * b:128 * b + 128, :] += part[:, 128 * (j - i):128 * (j - i) + 128]
    for side in (0, 1):
        for copy in stage[side] + direct[side] + forward[side]:
            copy.wait_send()


def rows(s, gram=True, chunks=4, hw=False, cid=0):
    R = s.shape[0] // 4
    return pl.pallas_call(
        functools.partial(rows_kernel, gram=gram, chunks=chunks, hw=hw),
        out_shape=(jax.ShapeDtypeStruct((4, R, 128), jnp.bfloat16), jax.ShapeDtypeStruct((1280, 128), F32)),
        in_specs=[pl.BlockSpec(memory_space=pl.ANY)],
        out_specs=(pl.BlockSpec(memory_space=pltpu.VMEM),) * 2,
        scratch_shapes=[
            pltpu.VMEM((2, chunks // 2, R // chunks, 128), jnp.bfloat16),
            pltpu.SemaphoreType.DMA((2, 2 * chunks)),
            pltpu.SemaphoreType.DMA((2, 2 * chunks)),
            pltpu.SemaphoreType.DMA,
        ],
        compiler_params=pltpu.CompilerParams(collective_id=cid, has_side_effects=True, vmem_limit_bytes=VLIM),
    )(s)


def sum_kernel(g_ref, out_ref, from_core, halves, from_plane, column, send, recv, *, parts=PARTS):
    core, x, y, z = where_am_i()
    sibling = device(1 - core, x, y, z)
    plane = [(d, lax.rem(x + d // 4, 4), lax.rem(y + d % 4, 4)) for d in range(1, 16)]
    line = [(d, lax.rem(z + d, 8)) for d in range(1, 8)]
    greet([sibling] + [device(core, px, py, z) for _, px, py in plane] + [device(core, x, y, pz) for _, pz in line])
    q = x * 4 + y

    def sizes(p):
        start, rows_ = parts[p]
        half = rows_ // 2
        return start, half, half // 16, start // 2

    each = range(len(parts))
    swap = []
    for p in each:
        start, half, piece, hs = sizes(p)
        swap.append(remote(g_ref.at[at(start + (1 - core) * half, half)], from_core.at[pl.ds(hs, half)],
                           send.at[p, 0, 0], recv.at[p, 0, 0], sibling))
        swap[p].start()
    spread = []
    for p in each:
        start, half, piece, hs = sizes(p)
        swap[p].wait_recv()
        halves[pl.ds(hs, half), :] = g_ref[at(start + core * half, half), :] + from_core[pl.ds(hs, half), :]
        spread.append([remote(halves.at[at(hs + (px * 4 + py) * piece, piece)], from_plane.at[d, pl.ds(hs // 16, piece)],
                              send.at[p, 1, d], recv.at[p, 1, d], device(core, px, py, z)) for d, px, py in plane])
        for copy in spread[p]:
            copy.start()
    ring = []
    for p in each:
        start, half, piece, hs = sizes(p)
        total = halves[at(hs + q * piece, piece), :]
        for (d, _, _), copy in zip(plane, spread[p]):
            copy.wait_recv()
            total = total + from_plane[d, pl.ds(hs // 16, piece), :]
        column[z, pl.ds(hs // 16, piece), :] = total
        mine = column.at[z, pl.ds(hs // 16, piece)]
        ring.append([remote(mine, mine, send.at[p, 2, d], recv.at[p, 2, d], device(core, x, y, pz)) for d, pz in line])
        for copy in ring[p]:
            copy.start()
    back = []
    for p in each:
        start, half, piece, hs = sizes(p)
        for copy in ring[p]:
            copy.wait_recv()
        total = column[0, pl.ds(hs // 16, piece), :]
        for k in range(1, 8):
            total = total + column[k, pl.ds(hs // 16, piece), :]
        own = at(start + core * half + q * piece, piece)
        out_ref[own, :] = total
        back.append([remote(out_ref.at[own], out_ref.at[own], send.at[p, 3, d], recv.at[p, 3, d], device(core, px, py, z))
                     for d, px, py in plane])
        for copy in back[p]:
            copy.start()
    last = []
    for p in each:
        start, half, piece, hs = sizes(p)
        for copy in back[p]:
            copy.wait_recv()
        mine = out_ref.at[at(start + core * half, half)]
        last.append(remote(mine, mine, send.at[p, 4, 0], recv.at[p, 4, 0], sibling))
        last[p].start()
    for p in each:
        last[p].wait_recv()
        for copy in [swap[p], last[p]] + spread[p] + ring[p] + back[p]:
            copy.wait_send()


def allsum(g, cid=1, parts=PARTS):
    rows_ = sum(n for _, n in parts)
    return pl.pallas_call(
        functools.partial(sum_kernel, parts=parts),
        out_shape=jax.ShapeDtypeStruct((rows_, 128), F32),
        in_specs=[pl.BlockSpec(memory_space=pltpu.VMEM)],
        out_specs=pl.BlockSpec(memory_space=pltpu.VMEM),
        scratch_shapes=[
            pltpu.VMEM((rows_ // 2, 128), F32),
            pltpu.VMEM((rows_ // 2, 128), F32),
            pltpu.VMEM((16, rows_ // 32, 128), F32),
            pltpu.VMEM((8, rows_ // 32, 128), F32),
            pltpu.SemaphoreType.DMA((len(parts), 5, 16)),
            pltpu.SemaphoreType.DMA((len(parts), 5, 16)),
        ],
        compiler_params=pltpu.CompilerParams(collective_id=cid, has_side_effects=True, vmem_limit_bytes=VLIM),
    )(g)


def out_kernel(rows_ref, w_ref, e_ref, basis_ref, energy_ref, sent, got, send, recv, *, chunks=4):
    core, x, y, z = where_am_i()
    R = rows_ref.shape[1]
    n = R // chunks
    peers = [(k, lax.rem(y + k, 4)) for k in (2, 1, 3)]
    greet([device(core, x, py, z) for _, py in peers])
    copies = []
    for c in range(chunks):
        block = jnp.concatenate([rows_ref[j, pl.ds(c * n, n), :] for j in range(4)], axis=1)
        part = lax.dot_general(w_ref[...], block, (((0,), (1,)), ((), ())), preferred_element_type=F32)
        part = part.astype(jnp.bfloat16)
        for j in range(4):
            sent[j, :, pl.ds(c * n, n)] = part[32 * j:32 * j + 32, :]
        for k, py in peers:
            copies.append(remote(sent.at[py, :, pl.ds(c * n, n)], got.at[y, :, pl.ds(c * n, n)],
                                 send.at[k, c], recv.at[k, c], device(core, x, py, z)))
            copies[-1].start()
    basis_ref[:, at(y * R, R, 128)] = sent[y].astype(F32)
    energy = jnp.zeros((1, 32), F32)
    for j in range(4):
        energy = jnp.where(y == j, e_ref[0:1, 32 * j:32 * j + 32], energy)
    energy_ref[...] = energy
    for copy in copies:
        copy.wait_recv()
    for k, _ in peers:
        source = lax.rem(y + 4 - k, 4)
        basis_ref[:, at(source * R, R, 128)] = got[source].astype(F32)
    for copy in copies:
        copy.wait_send()


def output(rows_, w, e, cid=2, chunks=4):
    R = rows_.shape[1]
    return pl.pallas_call(
        functools.partial(out_kernel, chunks=chunks),
        out_shape=(jax.ShapeDtypeStruct((32, 4 * R), F32), jax.ShapeDtypeStruct((1, 32), F32)),
        in_specs=[pl.BlockSpec(memory_space=pltpu.VMEM)] * 3,
        out_specs=(pl.BlockSpec(memory_space=pltpu.VMEM),) * 2,
        scratch_shapes=[
            pltpu.VMEM((4, 32, R), jnp.bfloat16),
            pltpu.VMEM((4, 32, R), jnp.bfloat16),
            pltpu.SemaphoreType.DMA((4, chunks)),
            pltpu.SemaphoreType.DMA((4, chunks)),
        ],
        compiler_params=pltpu.CompilerParams(collective_id=cid, has_side_effects=True, vmem_limit_bytes=VLIM),
    )(rows_, w, e)


HI = lax.Precision.HIGHEST


def dot(a, b, ca, cb, precision=HI):
    return lax.dot_general(a, b, (((ca,), (cb,)), ((), ())), precision=precision,
                           preferred_element_type=F32)


def inverse_cholesky(mats, outer=4):
    n = 128
    lane = lax.broadcasted_iota(jnp.int32, (8, n), 1)
    sub = lax.broadcasted_iota(jnp.int32, (8, n), 0)
    S = [[a[8 * r:8 * r + 8, :] for r in range(n // 8)] for a in mats]
    M = range(len(mats))
    panels = n // 8 // outer
    for panel in range(panels):
        first, last = outer * panel, outer * (panel + 1)
        for p in range(first, last):
            base = 8 * p
            inblock = (lane >= base) & (lane < base + 8)
            E = [[[jnp.broadcast_to(S[m][r][:, base + j:base + j + 1], (8, n)) for r in range(p, last)]
                  for j in range(8)] for m in M]
            for m in M:
                for r in range(p, last):
                    fill = jnp.where(lane - base == sub, 1.0, 0.0) if r == p else 0.0
                    S[m][r] = jnp.where(inblock, fill, S[m][r])
            scale = [jnp.zeros((8, n), F32) for m in M]
            for k in range(8):
                inv = [1.0 / jnp.broadcast_to(E[m][k][0][k:k + 1, :], (8, n)) for m in M]
                for m in M:
                    scale[m] = jnp.where(sub == k, inv[m], scale[m])
                    rows = [jnp.broadcast_to(E[m][j][0][k:k + 1, :], (8, n)) for j in range(k + 1, 8)]
                    pivot_row = jnp.broadcast_to(S[m][p][k:k + 1, :], (8, n))
                    for i, r in enumerate(range(p, last)):
                        mult = E[m][k][i] * inv[m]
                        if r == p:
                            mult = jnp.where(sub > k, mult, 0.0)
                        for j in range(k + 1, 8):
                            E[m][j][i] = E[m][j][i] - mult * rows[j - k - 1]
                        S[m][r] = S[m][r] - mult * pivot_row
            for m in M:
                S[m][p] = S[m][p] * jnp.sqrt(scale[m])
        if last < n // 8:
            for m in M:
                left = jnp.concatenate([jnp.where(lane >= 8 * last, S[m][p], 0.0) for p in range(first, last)], axis=0)
                right = jnp.concatenate(
                    [jnp.where((lane >= 8 * last) | (lane < 8 * p + 8), S[m][p], 0.0) for p in range(first, last)], axis=0)
                update = dot(left, right, 0, 0)
                outside = (lane < 8 * first) | (lane >= 8 * last)
                for r in range(last, n // 8):
                    S[m][r] = jnp.where(outside, S[m][r], 0.0) - update[8 * r:8 * r + 8, :]
    out = []
    for m in M:
        out.append(jnp.concatenate(
            [jnp.where(lane <= sub + 8 * r, S[m][r], 0.0) for r in range(n // 8)], axis=0))
    return out


def level(g_refs, x_ref, outer=4):
    half = F32(0.5 ** 0.5)
    row = lax.broadcasted_iota(jnp.int32, (256, 128), 0)
    col = lax.broadcasted_iota(jnp.int32, (256, 128), 1)
    start = jnp.where((row == col) | (row == col + 128), half, F32(0.0))
    for m in range(len(g_refs)):
        x_ref[m] = start

    def sweep(_, carry):
        ys = [dot(g[...], x_ref[m], 1, 0) for m, g in enumerate(g_refs)]
        inner = [dot(y, y, 0, 0) for y in ys]
        linv = inverse_cholesky(inner, outer)
        for m, y in enumerate(ys):
            x_ref[m] = dot(y, linv[m], 1, 1)
        return carry

    lax.fori_loop(0, 3, sweep, 0)
    return [x_ref[m].astype(jnp.bfloat16).astype(F32) for m in range(len(g_refs))]


def chain_kernel(blocks_ref, w_ref, e_ref, x_ref, g1_ref, g_ref, outer=4):
    for b, (i, j) in enumerate(PAIRS):
        block = blocks_ref[128 * b:128 * b + 128, :]
        g_ref[128 * i:128 * i + 128, 128 * j:128 * j + 128] = block
        if (i, j) in ((0, 1), (2, 3)):
            g_ref[128 * j:128 * j + 128, 128 * i:128 * i + 128] = block.T
    f0, f1 = level([g_ref.at[0:256, 0:256], g_ref.at[256:512, 256:512]], x_ref, outer)
    b0 = dot(g_ref[0:256, 0:256], f0, 1, 0)
    b01 = dot(g_ref[0:256, 256:512], f1, 1, 0)
    b1 = dot(g_ref[256:512, 256:512], f1, 1, 0)
    c01 = dot(f0, b01, 0, 0)
    g1_ref[0:128, 0:128] = dot(f0, b0, 0, 0)
    g1_ref[0:128, 128:256] = c01
    g1_ref[128:256, 0:128] = c01.T
    g1_ref[128:256, 128:256] = dot(f1, b1, 0, 0)
    f, = level([g1_ref], x_ref, outer)
    squares = jnp.sum(f * dot(g1_ref[...], f, 1, 0), axis=0, keepdims=True)
    energies = jnp.sqrt(squares + 1e-6)
    e_ref[...] = jnp.broadcast_to(energies, (8, 128))
    inv = 1.0 / energies
    w_ref[0:256, :] = (dot(f0, f[0:128], 1, 0) * inv).astype(jnp.bfloat16)
    w_ref[256:512, :] = (dot(f1, f[128:256], 1, 0) * inv).astype(jnp.bfloat16)


def chain(g, outer=4):
    return pl.pallas_call(
        functools.partial(chain_kernel, outer=outer),
        out_shape=(jax.ShapeDtypeStruct((512, 128), jnp.bfloat16), jax.ShapeDtypeStruct((8, 128), F32)),
        in_specs=[pl.BlockSpec(memory_space=pltpu.VMEM)],
        out_specs=(pl.BlockSpec(memory_space=pltpu.VMEM),) * 2,
        scratch_shapes=[pltpu.VMEM((2, 256, 128), F32), pltpu.VMEM((256, 256), F32),
                        pltpu.VMEM((512, 512), F32)],
        compiler_params=pltpu.CompilerParams(vmem_limit_bytes=32 * 1024 * 1024),
    )(g)


def body(snapshots):
    own_rows, gram = rows(snapshots)
    gram = allsum(gram)
    weights, lengths = chain(gram)
    basis, energies = output(own_rows, weights, lengths)
    return basis.T, energies.reshape(32)


def solution(mesh):
    return jax.shard_map(body, mesh=mesh, in_specs=(P("wide", "narrow"),), out_specs=(P("wide", "narrow"), P("narrow")),
                         check_vma=False)
```

time: 831 us -> 111 us (0.13)
  waiting for transfers between devices: 498 us -> 0 us
  other arithmetic: 146 us -> 0 us
  blocking collectives: 131 us -> 0 us
  Pallas kernels: 0 us -> 107 us
  matrix products: 25 us -> 0 us
  between operations: 14.3 us -> 0.67 us
    psum x3 -> x0, waiting for transfers between devices: 405 us -> none  [the longest x2 351 us: body(): gram_sum = lax.psum(local_gram, 'wide')]
    another operation x31 -> x0, other arithmetic: 137 us -> none  [the longest x19 74.3 us: orthonormal(): lower_factor = jnp.linalg.cholesky(inner)]
    psum x2 -> x0, blocking collectives: 131 us -> none  [the longest x1 123 us: body(): squares = lax.psum(jnp.sum(current * current, axis=0), 'wide')]
    pallas_call x0 -> x4, Pallas kernels: none -> 107 us  [the longest x1 35.1 us: chain(): pl.pallas_call(functools.partial(chain_kernel, outer=outer), out_shape=(j...]
    ppermute x2 -> x0, waiting for transfers between devices: 93.2 us -> none  [shifted(): lax.ppermute(value, axis, [(source, source + steps) for source in range(f...]
    dot_general x16 -> x0, matrix products: 23.2 us -> none  [the longest x2 8.93 us: body(): merged = jnp.dot(paired, factor, preferred_element_type=jnp.float32)]
  transfers between devices with their start and end apart: 5 -> 0, of which waited for: 5 -> 0; matrix products, arithmetic and copies ran while one was open for 0% -> 0% of each run, Pallas kernels for 0% -> 0%
where the time goes in v1:
time: 111 us
  Pallas kernels  107 us (96%)
  local copies, waits for them, and re-layouts  3.07 us (3%)
    pallas_call x1, Pallas kernels, chain(): pl.pallas_call(functools.partial(chain_kernel, outer=outer), out_shape=(j...  35.1 us
    pallas_call x1, Pallas kernels, allsum(): pl.pallas_call(functools.partial(sum_kernel, parts=parts), out_shape=jax....  34.3 us
    pallas_call x1, Pallas kernels, rows(): pl.pallas_call(functools.partial(rows_kernel, gram=gram, chunks=chunks, h...  27.5 us
    pallas_call x1, Pallas kernels, output(): pl.pallas_call(functools.partial(out_kernel, chunks=chunks), out_shape=(j...  10.4 us
    unnamed x4, local copies, waits for them, and re-layouts  3.07 us

profile of v1, /device:TPU:1, one launch (start us, length us, event | category | flops | bytes accessed | tf_op | source)
XLA Modules:
  0.0 111.0 jit_solution(11645668513473177933)
XLA Ops:
  0.6 0.0 copy-start
  0.6 1.6 %copy-done = bf16[8192,128]{1,0:T(8,128)(2,1)S(1)} copy-done((bf16[8192,128]{1,0:T(8,128)(2,1)S(1)}, bf16[8192,128]{1,0:T(8,128)(2,1)}, u32[]{:S(2)}) %copy-start) | copy-done | bytes 2097176
  2.2 27.5 %shard_map.30 = (bf16[4,2048,128]{2,1,0:T(8,128)(2,1)S(1)}, f32[1280,128]{1,0:T(8,128)S(1)}) custom-call(bf16[8192,128]{1,0:T(8,128)(2,1)S(1)} %copy-done), custom_call_target="tpu_custom_call" | custom-call | tf_op jit(solution)/shard_map/pallas_call | solution.py:104
  29.7 34.3 %shard_map.31.blocks_ref = f32[1280,128]{1,0:T(8,128)S(1)} custom-call(f32[1280,128]{1,0:T(8,128)S(1)} %get-tuple-element.9.g_ref), custom_call_target="tpu_custom_call" | custom-call | tf_op jit(solution)/shard_map/pallas_call | solution.py:190
  64.0 35.1 %shard_map.32 = (bf16[512,128]{1,0:T(8,128)(2,1)S(1)}, f32[8,128]{1,0:T(8,128)S(1)}) custom-call(f32[1280,128]{1,0:T(8,128)S(1)} %shard_map.31.blocks_ref), custom_call_target="tpu_custom_call" | custom-call | tf_op jit(solution)/shard_map/pallas_call | solution.py:358
  99.1 10.4 %shard_map.33 = (f32[32,8192]{1,0:T(8,128)S(1)}, f32[1,32]{1,0:T(1,128)S(1)}) custom-call(bf16[4,2048,128]{2,1,0:T(8,128)(2,1)S(1)} %get-tuple-element.8.rows_ref, bf16[512,128]{1,0:T(8,128)(2,1)S(1)} %get-tuple-element.10.w_ref, f32[8,128]{1,0:T(8,128)S(1)} %get-tuple-element.11.e_ref), custom_call_target="tpu_custom_call" | custom-call | tf_op jit(solution)/shard_map/pallas_call | solution.py:240
  109.5 1.0 copy.5
  110.5 0.5 copy.6
Async XLA Ops:
  0.6 1.6 %copy-start = (bf16[8192,128]{1,0:T(8,128)(2,1)S(1)}, bf16[8192,128]{1,0:T(8,128)(2,1)}, u32[]{:S(2)}) copy-start(bf16[8192,128]{1,0:T(8,128)(2,1)} %s_ref.1) | copy-start | bytes 6291460

commit v2 on v0

v2 whole, which is shorter than its diff:
```python
import functools

import jax
import jax.numpy as jnp
from jax import lax
from jax.experimental import pallas as pl
from jax.experimental.pallas import tpu as pltpu
from jax.sharding import PartitionSpec as P

MESH = pl.DeviceIdType.MESH
HI = lax.Precision.HIGHEST
F32 = jnp.float32
BF16 = jnp.bfloat16
SWEEPS = 3
EPSILON = 1e-6
BLOCKS = ((0, 0), (0, 1), (1, 1), (2, 2), (2, 3), (3, 3), (0, 2), (0, 3), (1, 2), (1, 3))
PARTS = ((0, 768), (768, 512))
CHUNKS = 4


def dot(a, b, ca, cb, precision=HI):
    return lax.dot_general(a, b, (((ca,), (cb,)), ((), ())), precision=precision, preferred_element_type=F32)


def inverse_cholesky(mats, outer=4, wide=2):
    n = 128
    lane = lax.broadcasted_iota(jnp.int32, (8, n), 1)
    sub = lax.broadcasted_iota(jnp.int32, (8, n), 0)
    S = [[a[8 * r:8 * r + 8, :] for r in range(n // 8)] for a in mats]
    M = range(len(mats))
    full = lambda row: jnp.broadcast_to(row, (8, n))
    for first in range(0, n // 8, outer):
        last = first + outer
        for p in range(first, last, wide):
            base = 8 * p
            inblock = (lane >= base) & (lane < base + 8 * wide)
            E = [[{r: full(S[m][r][:, base + j:base + j + 1]) for r in range(p + j // 8, last)}
                  for j in range(8 * wide)] for m in M]
            for m in M:
                for r in range(p, last):
                    fill = jnp.where(lane - 8 * r == sub, 1.0, 0.0) if r < p + wide else 0.0
                    S[m][r] = jnp.where(inblock, fill, S[m][r])
            scale = [[jnp.zeros((8, n), F32)] * wide for m in M]
            for k in range(8 * wide):
                top, row = p + k // 8, k % 8
                inv = [1.0 / full(E[m][k][top][row:row + 1, :]) for m in M]
                for m in M:
                    scale[m][k // 8] = jnp.where(sub == row, inv[m], scale[m][k // 8])
                    pivots = {j: full(E[m][k][p + j // 8][j % 8:j % 8 + 1, :]) for j in range(k + 1, 8 * wide)}
                    pivot_row = full(S[m][top][row:row + 1, :])
                    for r in range(top, last):
                        mult = E[m][k][r] * inv[m]
                        if r == top:
                            mult = jnp.where(sub > row, mult, 0.0)
                        for j in range(k + 1, 8 * wide):
                            if r >= p + j // 8:
                                E[m][j][r] = E[m][j][r] - mult * pivots[j]
                        S[m][r] = S[m][r] - mult * pivot_row
            for m in M:
                for i in range(wide):
                    S[m][p + i] = S[m][p + i] * jnp.sqrt(scale[m][i])
        if last < n // 8:
            for m in M:
                left = jnp.concatenate([jnp.where(lane >= 8 * last, S[m][p], 0.0) for p in range(first, last)], axis=0)
                right = jnp.concatenate(
                    [jnp.where((lane >= 8 * last) | (lane < 8 * (p - (p - first) % wide + wide)), S[m][p], 0.0)
                     for p in range(first, last)], axis=0)
                update = dot(left, right, 0, 0)
                outside = (lane < 8 * first) | (lane >= 8 * last)
                for r in range(last, n // 8):
                    S[m][r] = jnp.where(outside, S[m][r], 0.0) - update[8 * r:8 * r + 8, :]
    return [jnp.concatenate([jnp.where(lane <= sub + 8 * r, S[m][r], 0.0) for r in range(n // 8)], axis=0) for m in M]


def device(core, x, y, z):
    return {"wide": (z * 4 + x) * 2 + core, "narrow": y}


def remote(src, dst, send, recv, peer):
    return pltpu.make_async_remote_copy(src_ref=src, dst_ref=dst, send_sem=send, recv_sem=recv,
                                        device_id=peer, device_id_type=MESH)


def at(start, size, align=8):
    return pl.ds(pl.multiple_of(start, align), size)


def start_all(copies):
    for copy in copies:
        copy.start()
    return copies


def level(grams, y_ref, between=None):
    for m, g in enumerate(grams):
        y_ref[m] = (g[:, 0:128] + g[:, 128:256]) * F32(0.5 ** 0.5)

    def sweep(step, carry):
        ys = [y_ref[m] for m in range(len(grams))]
        linv = inverse_cholesky([dot(v, v, 0, 0) for v in ys])
        ahead = [jnp.where(step == SWEEPS - 1, v, dot(g[...], v, 1, 0)) for g, v in zip(grams, ys)]
        for m, v in enumerate(ahead):
            y_ref[m] = dot(v, linv[m], 1, 1)
        if between is not None:
            between(step)
        return carry

    lax.fori_loop(0, SWEEPS, sweep, 0)
    return [y_ref[m].astype(BF16).astype(F32) for m in range(len(grams))]


def kernel(s_ref, basis_ref, energy_ref, rows_ref, part_ref, sum_ref, from_core, halves, from_plane, column,
           g_ref, g1_ref, x_ref, sent_ref, got_ref,
           own_sem, row_send, row_recv, sum_send, sum_recv, out_send, out_recv):
    w = lax.axis_index("wide")
    y = lax.axis_index("narrow")
    core, x, z = lax.rem(w, 2), lax.rem(lax.div(w, 2), 4), lax.div(w, 8)
    R = rows_ref.shape[1]
    n = R // CHUNKS
    sibling = device(1 - core, x, y, z)
    plane = [(d, lax.rem(x + d // 4, 4), lax.rem(y + d % 4, 4)) for d in range(1, 16)]
    line = [(d, lax.rem(z + d, 8)) for d in range(1, 8)]

    barrier = pltpu.get_barrier_semaphore()
    peers = [device(core, x, y, pz) for d, pz in sorted(line, key=lambda v: abs(v[0] - 4))]
    peers += [device(core, px, py, z) for d, px, py in sorted(plane, key=lambda v: abs(v[0] // 4 - 2) + abs(v[0] % 4 - 2))]
    peers += [sibling]
    for peer in peers:
        pl.semaphore_signal(barrier, inc=1, device_id=peer, device_id_type=MESH)
    own = pltpu.make_async_copy(s_ref.at[at(y * R, R, 16)], rows_ref.at[y], own_sem)
    own.start()
    part_ref[...] = jnp.zeros_like(part_ref)
    pl.semaphore_wait(barrier, len(peers))

    moves = []
    for c in range(CHUNKS):
        moves.append([])
        for k in (2, 1, 3):
            py = lax.rem(y + k, 4)
            moves[c].append(remote(s_ref.at[at(py * R + c * n, n, 16)], rows_ref.at[y, pl.ds(c * n, n)],
                                   row_send.at[k, c], row_recv.at[k, c], device(core, x, py, z)))
        start_all(moves[c])
    own.wait()
    for c in range(CHUNKS):
        for copy in moves[c]:
            copy.wait_recv()
        blocks = [rows_ref[j, pl.ds(c * n, n), :] for j in range(4)]
        for i in range(4):
            part = dot(blocks[i], jnp.concatenate(blocks[i:], axis=1), 0, 0, None)
            for j in range(i, 4):
                b = BLOCKS.index((i, j))
                part_ref[128 * b:128 * b + 128, :] += part[:, 128 * (j - i):128 * (j - i) + 128]

    q = x * 4 + y

    def sizes(p):
        start, length = PARTS[p]
        return start, length // 2, length // 32, start // 2

    def swap(p):
        start, half, piece, hs = sizes(p)
        return remote(part_ref.at[at(start + (1 - core) * half, half)], from_core.at[pl.ds(hs, half)],
                      sum_send.at[p, 0, 0], sum_recv.at[p, 0, 0], sibling)

    def spread(p):
        start, half, piece, hs = sizes(p)
        return [remote(halves.at[at(hs + (px * 4 + py) * piece, piece)], from_plane.at[d, pl.ds(hs // 16, piece)],
                       sum_send.at[p, 1, d], sum_recv.at[p, 1, d], device(core, px, py, z)) for d, px, py in plane]

    def ring(p):
        start, half, piece, hs = sizes(p)
        mine = column.at[z, pl.ds(hs // 16, piece)]
        return [remote(mine, mine, sum_send.at[p, 2, d], sum_recv.at[p, 2, d], device(core, x, y, pz)) for d, pz in line]

    def back(p):
        start, half, piece, hs = sizes(p)
        mine = sum_ref.at[at(start + core * half + q * piece, piece)]
        return [remote(mine, mine, sum_send.at[p, 3, d], sum_recv.at[p, 3, d], device(core, px, py, z))
                for d, px, py in plane]

    def last(p):
        start, half, piece, hs = sizes(p)
        mine = sum_ref.at[at(start + core * half, half)]
        return remote(mine, mine, sum_send.at[p, 4, 0], sum_recv.at[p, 4, 0], sibling)

    def after_swap(p):
        start, half, piece, hs = sizes(p)
        swap(p).wait_recv()
        halves[pl.ds(hs, half), :] = part_ref[at(start + core * half, half), :] + from_core[pl.ds(hs, half), :]
        start_all(spread(p))

    def after_spread(p):
        start, half, piece, hs = sizes(p)
        total = halves[at(hs + q * piece, piece), :]
        for (d, _, _), copy in zip(plane, spread(p)):
            copy.wait_recv()
            total = total + from_plane[d, pl.ds(hs // 16, piece), :]
        column[z, pl.ds(hs // 16, piece), :] = total
        start_all(ring(p))

    def after_ring(p):
        start, half, piece, hs = sizes(p)
        for copy in ring(p):
            copy.wait_recv()
        total = column[0, pl.ds(hs // 16, piece), :]
        for k in range(1, 8):
            total = total + column[k, pl.ds(hs // 16, piece), :]
        sum_ref[at(start + core * half + q * piece, piece), :] = total
        start_all(back(p))

    def after_back(p):
        for copy in back(p):
            copy.wait_recv()
        last(p).start()

    def after_last(p):
        last(p).wait_recv()
        for b, (i, j) in enumerate(BLOCKS):
            if PARTS[p][0] <= 128 * b < sum(PARTS[p]):
                block = sum_ref[128 * b:128 * b + 128, :]
                g_ref[128 * i:128 * i + 128, 128 * j:128 * j + 128] = block
                if p == 0 and i != j:
                    g_ref[128 * j:128 * j + 128, 128 * i:128 * i + 128] = block.T

    swap(0).start()
    swap(1).start()
    after_swap(0)
    after_spread(0)
    after_swap(1)
    after_ring(0)
    after_spread(1)
    after_back(0)
    after_last(0)

    def between(step):
        for k, go_on in enumerate((after_ring, after_back)):
            @pl.when(step == k)
            def _():
                go_on(1)

    f0, f1 = level([g_ref.at[0:256, 0:256], g_ref.at[256:512, 256:512]], x_ref, between)
    g1_ref[0:128, 0:128] = dot(f0, dot(g_ref[0:256, 0:256], f0, 1, 0), 0, 0)
    g1_ref[128:256, 128:256] = dot(f1, dot(g_ref[256:512, 256:512], f1, 1, 0), 0, 0)
    after_last(1)
    cross = dot(f0, dot(g_ref[0:256, 256:512], f1, 1, 0), 0, 0)
    g1_ref[0:128, 128:256] = cross
    g1_ref[128:256, 0:128] = cross.T
    f, = level([g1_ref], x_ref)
    squares = jnp.sum(f * dot(g1_ref[...], f, 1, 0), axis=0, keepdims=True)
    energies = jnp.sqrt(squares + EPSILON)
    share = jnp.zeros((1, 32), F32)
    for j in range(4):
        share = jnp.where(y == j, energies[:, 32 * j:32 * j + 32], share)
    energy_ref[...] = share
    f = f * (1.0 / energies)
    weights = jnp.concatenate([dot(f[0:128], f0, 0, 1), dot(f[128:256], f1, 0, 1)], axis=1).astype(BF16)

    shares = []
    for c in range(CHUNKS):
        block = jnp.concatenate([rows_ref[j, pl.ds(c * n, n), :] for j in range(4)], axis=1)
        part = dot(weights, block, 1, 1, None).astype(BF16)
        for j in range(4):
            sent_ref[j, :, pl.ds(c * n, n)] = part[32 * j:32 * j + 32, :]
        for k in (2, 1, 3):
            py = lax.rem(y + k, 4)
            shares.append((py, c, remote(sent_ref.at[py, :, pl.ds(c * n, n)], got_ref.at[y, :, pl.ds(c * n, n)],
                                 out_send.at[k, c], out_recv.at[k, c], device(core, x, py, z))))
            shares[-1][-1].start()
    basis_ref[:, at(y * R, R, 128)] = sent_ref[y].astype(F32)
    for k in (1, 3, 2):
        for c in range(CHUNKS):
            py = lax.rem(y + k, 4)
            remote(got_ref.at[py, :, pl.ds(c * n, n)], got_ref.at[py, :, pl.ds(c * n, n)],
                   out_send.at[4 - k, c], out_recv.at[4 - k, c], device(core, x, py, z)).wait_recv()
            basis_ref[:, at(py * R + c * n, n, 128)] = got_ref[py, :, pl.ds(c * n, n)].astype(F32)
    for copies in moves:
        for copy in copies:
            copy.wait_send()
    for p in range(len(PARTS)):
        for copy in [swap(p), last(p)] + spread(p) + ring(p) + back(p):
            copy.wait_send()
    for _, c, copy in shares:
        copy.wait_send()


def body(snapshots):
    R = snapshots.shape[0] // 4
    total = sum(length for _, length in PARTS)
    basis, energies = pl.pallas_call(
        kernel,
        out_shape=(jax.ShapeDtypeStruct((32, 4 * R), F32), jax.ShapeDtypeStruct((1, 32), F32)),
        in_specs=[pl.BlockSpec(memory_space=pl.ANY)],
        out_specs=(pl.BlockSpec(memory_space=pltpu.VMEM),) * 2,
        scratch_shapes=[
            pltpu.VMEM((4, R, 128), BF16),
            pltpu.VMEM((total, 128), F32),
            pltpu.VMEM((total, 128), F32),
            pltpu.VMEM((total // 2, 128), F32),
            pltpu.VMEM((total // 2, 128), F32),
            pltpu.VMEM((16, total // 32, 128), F32),
            pltpu.VMEM((8, total // 32, 128), F32),
            pltpu.VMEM((512, 512), F32),
            pltpu.VMEM((256, 256), F32),
            pltpu.VMEM((2, 256, 128), F32),
            pltpu.VMEM((4, 32, R), BF16),
            pltpu.VMEM((4, 32, R), BF16),
            pltpu.SemaphoreType.DMA,
            pltpu.SemaphoreType.DMA((4, CHUNKS)),
            pltpu.SemaphoreType.DMA((4, CHUNKS)),
            pltpu.SemaphoreType.DMA((2, 5, 16)),
            pltpu.SemaphoreType.DMA((2, 5, 16)),
            pltpu.SemaphoreType.DMA((4, CHUNKS)),
            pltpu.SemaphoreType.DMA((4, CHUNKS)),
        ],
        compiler_params=pltpu.CompilerParams(collective_id=0, has_side_effects=True, vmem_limit_bytes=60 * 1024 * 1024),
    )(snapshots)
    return basis.T, energies.reshape(32)


def solution(mesh):
    return jax.shard_map(body, mesh=mesh, in_specs=(P("wide", "narrow"),), out_specs=(P("wide", "narrow"), P("narrow")),
                         check_vma=False)
```

time: 831 us -> 102 us (0.12)
  waiting for transfers between devices: 498 us -> 0 us
  other arithmetic: 146 us -> 0 us
  blocking collectives: 131 us -> 0 us
  Pallas kernels: 0 us -> 98 us
  matrix products: 25 us -> 0 us
  between operations: 14.3 us -> 0.65 us
    psum x3 -> x0, waiting for transfers between devices: 405 us -> none  [the longest x2 351 us: body(): gram_sum = lax.psum(local_gram, 'wide')]
    another operation x31 -> x0, other arithmetic: 137 us -> none  [the longest x19 74.3 us: orthonormal(): lower_factor = jnp.linalg.cholesky(inner)]
    psum x2 -> x0, blocking collectives: 131 us -> none  [the longest x1 123 us: body(): squares = lax.psum(jnp.sum(current * current, axis=0), 'wide')]
    pallas_call x0 -> x1, Pallas kernels: none -> 98 us  [body(): pl.pallas_call(kernel, out_shape=(jax.ShapeDtypeStruct((32, 4 * R), F32),...]
    ppermute x2 -> x0, waiting for transfers between devices: 93.2 us -> none  [shifted(): lax.ppermute(value, axis, [(source, source + steps) for source in range(f...]
    dot_general x16 -> x0, matrix products: 23.2 us -> none  [the longest x2 8.93 us: body(): merged = jnp.dot(paired, factor, preferred_element_type=jnp.float32)]
  transfers between devices with their start and end apart: 5 -> 0, of which waited for: 5 -> 0; matrix products, arithmetic and copies ran while one was open for 0% -> 0% of each run, Pallas kernels for 0% -> 0%
where the time goes in v2:
time: 102 us; the launch traced here: 101 us
  Pallas kernels  98 us (96%)
  local copies, waits for them, and re-layouts  2.78 us (3%)
    pallas_call x1, Pallas kernels, body(): pl.pallas_call(kernel, out_shape=(jax.ShapeDtypeStruct((32, 4 * R), F32),...  98 us
    unnamed x4, local copies, waits for them, and re-layouts  2.78 us

profile of v2, /device:TPU:1, one launch (start us, length us, event | category | flops | bytes accessed | tf_op | source)
XLA Modules:
  0.0 101.4 jit_solution(10573755851513012414)
XLA Ops:
  0.6 98.0 %shard_map.30 = (f32[32,8192]{1,0:T(8,128)}, f32[1,32]{1,0:T(1,128)}) custom-call(bf16[8192,128]{1,0:T(8,128)(2,1)} %s_ref.1), custom_call_target="tpu_custom_call" | custom-call | tf_op jit(solution)/shard_map/pallas_call | solution.py:289
  98.6 0.0 copy-start
  98.6 2.3 %copy.5 = f32[8192,32]{0,1:T(8,128)} copy(f32[8192,32]{0,1:T(8,128)} %bitcast.2) | data formatting | bytes 2097152
  100.9 0.0 copy-done
  100.9 0.5 copy.6
Async XLA Ops:
  98.6 2.3 %copy-start = (f32[1,32]{1,0:T(1,128)S(1)}, f32[1,32]{1,0:T(1,128)}, u32[]{:S(2)}) copy-start(f32[1,32]{1,0:T(1,128)} %get-tuple-element.5) | copy-start | bytes 388

commit v3 on v2

v3 whole, which is shorter than its diff:
```python
import functools

import jax
import jax.numpy as jnp
from jax import lax
from jax.experimental import pallas as pl
from jax.experimental.pallas import tpu as pltpu
from jax.sharding import PartitionSpec as P

MESH = pl.DeviceIdType.MESH
HI = lax.Precision.HIGHEST
F32 = jnp.float32
BF16 = jnp.bfloat16
SWEEPS = 3
EPSILON = 1e-6
BLOCKS = ((0, 0), (0, 1), (1, 1), (2, 2), (2, 3), (3, 3), (0, 2), (0, 3), (1, 2), (1, 3))
PARTS = ((0, 768), (768, 512))
CHUNKS = 4


def dot(a, b, ca, cb, precision=HI):
    return lax.dot_general(a, b, (((ca,), (cb,)), ((), ())), precision=precision, preferred_element_type=F32)


def thirds(a):
    high = a.astype(BF16)
    rest = a - high.astype(F32)
    middle = rest.astype(BF16)
    return high, middle, (rest - middle.astype(F32)).astype(BF16)


def short_dot(a, b):
    ah, am, al = thirds(a)
    bh, bm, bl = thirds(b)
    left = jnp.concatenate([ah, ah, am, am, ah, al], axis=0)
    right = jnp.concatenate([bh, bm, bh, bm, bl, bh], axis=0)
    return lax.dot_general(left, right, (((0,), (0,)), ((), ())), preferred_element_type=F32)


def inverse_cholesky(mats, outer=4, wide=2):
    n = 128
    lane = lax.broadcasted_iota(jnp.int32, (8, n), 1)
    sub = lax.broadcasted_iota(jnp.int32, (8, n), 0)
    S = [[a[8 * r:8 * r + 8, :] for r in range(n // 8)] for a in mats]
    M = range(len(mats))
    inverse_pivots = [[] for m in M]
    full = lambda row: jnp.broadcast_to(row, (8, n))
    for first in range(0, n // 8, outer):
        last = first + outer
        for p in range(first, last, wide):
            base = 8 * p
            inblock = (lane >= base) & (lane < base + 8 * wide)
            E = [[{r: full(S[m][r][:, base + j:base + j + 1]) for r in range(p + j // 8, last)}
                  for j in range(8 * wide)] for m in M]
            for m in M:
                for r in range(p, last):
                    fill = jnp.where(lane - 8 * r == sub, 1.0, 0.0) if r < p + wide else 0.0
                    S[m][r] = jnp.where(inblock, fill, S[m][r])
            scale = [[jnp.zeros((8, n), F32)] * wide for m in M]
            for k in range(8 * wide):
                top, row = p + k // 8, k % 8
                inv = [1.0 / full(E[m][k][top][row:row + 1, :]) for m in M]
                for m in M:
                    scale[m][k // 8] = jnp.where(sub == row, inv[m], scale[m][k // 8])
                    pivots = {j: full(E[m][k][p + j // 8][j % 8:j % 8 + 1, :]) for j in range(k + 1, 8 * wide)}
                    pivot_row = full(S[m][top][row:row + 1, :])
                    for r in range(top, last):
                        mult = E[m][k][r] * inv[m]
                        if r == top:
                            mult = jnp.where(sub > row, mult, 0.0)
                        for j in range(k + 1, 8 * wide):
                            if r >= p + j // 8:
                                E[m][j][r] = E[m][j][r] - mult * pivots[j]
                        S[m][r] = S[m][r] - mult * pivot_row
            for m in M:
                inverse_pivots[m] += scale[m]
        if last < n // 8:
            for m in M:
                left = jnp.concatenate([jnp.where(lane >= 8 * last, S[m][p] * inverse_pivots[m][p], 0.0)
                                        for p in range(first, last)], axis=0)
                right = jnp.concatenate(
                    [jnp.where((lane >= 8 * last) | (lane < 8 * (p - (p - first) % wide + wide)), S[m][p], 0.0)
                     for p in range(first, last)], axis=0)
                update = short_dot(left, right)
                outside = (lane < 8 * first) | (lane >= 8 * last)
                for r in range(last, n // 8):
                    S[m][r] = jnp.where(outside, S[m][r], 0.0) - update[8 * r:8 * r + 8, :]
    return [jnp.concatenate([jnp.where(lane <= sub + 8 * r, S[m][r] * jnp.sqrt(inverse_pivots[m][r]), 0.0) for r in range(n // 8)], axis=0) for m in M]


def device(core, x, y, z):
    return {"wide": (z * 4 + x) * 2 + core, "narrow": y}


def remote(src, dst, send, recv, peer):
    return pltpu.make_async_remote_copy(src_ref=src, dst_ref=dst, send_sem=send, recv_sem=recv,
                                        device_id=peer, device_id_type=MESH)


def at(start, size, align=8):
    return pl.ds(pl.multiple_of(start, align), size)


def start_all(copies):
    for copy in copies:
        copy.start()


def arrived(like, sem):
    pltpu.make_async_copy(like, like, sem).wait()


def level(grams, y_ref, between=None):
    for m, g in enumerate(grams):
        y_ref[m] = (g[:, 0:128] + g[:, 128:256]) * F32(0.5 ** 0.5)

    def sweep(step, carry):
        ys = [y_ref[m] for m in range(len(grams))]
        linv = inverse_cholesky([dot(v, v, 0, 0) for v in ys])
        ahead = [jnp.where(step == SWEEPS - 1, v, dot(g[...], v, 1, 0)) for g, v in zip(grams, ys)]
        for m, v in enumerate(ahead):
            y_ref[m] = dot(v, linv[m], 1, 1)
        if between is not None:
            between(step)
        return carry

    lax.fori_loop(0, SWEEPS, sweep, 0)
    return [y_ref[m].astype(BF16).astype(F32) for m in range(len(grams))]


def kernel(s_ref, basis_ref, energy_ref, rows_ref, part_ref, sum_ref, from_core, halves, from_plane, column,
           g_ref, g1_ref, x_ref, sent_ref, got_ref,
           own_sem, row_send, row_recv, sum_send, sum_recv, out_send, out_recv):
    w = lax.axis_index("wide")
    y = lax.axis_index("narrow")
    core, x, z = lax.rem(w, 2), lax.rem(lax.div(w, 2), 4), lax.div(w, 8)
    n = rows_ref.shape[2]
    R = n * CHUNKS
    sibling = device(1 - core, x, y, z)
    plane = [(d, lax.rem(x + d // 4, 4), lax.rem(y + d % 4, 4)) for d in range(1, 16)]
    line = [(d, lax.rem(z + d, 8)) for d in range(1, 8)]

    barrier = pltpu.get_barrier_semaphore()
    peers = [device(core, x, y, pz) for d, pz in sorted(line, key=lambda v: abs(v[0] - 4))]
    peers += [device(core, px, py, z) for d, px, py in sorted(plane, key=lambda v: abs(v[0] // 4 - 2) + abs(v[0] % 4 - 2))]
    peers += [sibling]
    for peer in peers:
        pl.semaphore_signal(barrier, inc=1, device_id=peer, device_id_type=MESH)
    for c in range(CHUNKS):
        pltpu.make_async_copy(s_ref.at[at(y * R + c * n, n, 16)], rows_ref.at[c, y], own_sem).start()
    part_ref[...] = jnp.zeros_like(part_ref)
    pl.semaphore_wait(barrier, len(peers))

    for c in range(CHUNKS):
        for k in (2, 1, 3):
            py = lax.rem(y + k, 4)
            remote(s_ref.at[at(py * R + c * n, n, 16)], rows_ref.at[c, y], row_send, row_recv.at[c],
                   device(core, x, py, z)).start()
    arrived(rows_ref.at[0], own_sem)
    for c in range(CHUNKS):
        arrived(rows_ref.at[c, pl.ds(0, 3)], row_recv.at[c])
        blocks = [rows_ref[c, j] for j in range(4)]
        for i in range(4):
            part = dot(blocks[i], jnp.concatenate(blocks[i:], axis=1), 0, 0, None)
            for j in range(i, 4):
                b = BLOCKS.index((i, j))
                part_ref[128 * b:128 * b + 128, :] += part[:, 128 * (j - i):128 * (j - i) + 128]

    q = x * 4 + y

    def sizes(p):
        start, length = PARTS[p]
        return start, length // 2, length // 32, start // 2

    def swap(p):
        start, half, piece, hs = sizes(p)
        remote(part_ref.at[at(start + (1 - core) * half, half)], from_core.at[pl.ds(hs, half)],
               sum_send.at[p, 0], sum_recv.at[p, 0], sibling).start()

    def after_swap(p):
        start, half, piece, hs = sizes(p)
        arrived(from_core.at[pl.ds(hs, half)], sum_recv.at[p, 0])
        halves[pl.ds(hs, half), :] = part_ref[at(start + core * half, half), :] + from_core[pl.ds(hs, half), :]
        for d, px, py in plane:
            remote(halves.at[at(hs + (px * 4 + py) * piece, piece)], from_plane.at[d, pl.ds(hs // 16, piece)],
                   sum_send.at[p, 1], sum_recv.at[p, 1], device(core, px, py, z)).start()

    def after_spread(p):
        start, half, piece, hs = sizes(p)
        arrived(from_plane.at[pl.ds(1, 15), pl.ds(hs // 16, piece)], sum_recv.at[p, 1])
        total = halves[at(hs + q * piece, piece), :]
        for d in range(1, 16):
            total = total + from_plane[d, pl.ds(hs // 16, piece), :]
        mine = column.at[z, pl.ds(hs // 16, piece)]
        mine[...] = total
        for d, pz in line:
            remote(mine, mine, sum_send.at[p, 2], sum_recv.at[p, 2], device(core, x, y, pz)).start()

    def after_ring(p):
        start, half, piece, hs = sizes(p)
        arrived(column.at[pl.ds(0, 7), pl.ds(hs // 16, piece)], sum_recv.at[p, 2])
        total = column[0, pl.ds(hs // 16, piece), :]
        for k in range(1, 8):
            total = total + column[k, pl.ds(hs // 16, piece), :]
        mine = sum_ref.at[at(start + core * half + q * piece, piece)]
        mine[...] = total
        for d, px, py in plane:
            remote(mine, mine, sum_send.at[p, 3], sum_recv.at[p, 3], device(core, px, py, z)).start()

    def after_back(p):
        start, half, piece, hs = sizes(p)
        arrived(sum_ref.at[pl.ds(start, 15 * piece)], sum_recv.at[p, 3])
        mine = sum_ref.at[at(start + core * half, half)]
        remote(mine, mine, sum_send.at[p, 4], sum_recv.at[p, 4], sibling).start()

    def after_last(p):
        start, half, piece, hs = sizes(p)
        arrived(sum_ref.at[pl.ds(start, half)], sum_recv.at[p, 4])
        for b, (i, j) in enumerate(BLOCKS):
            if PARTS[p][0] <= 128 * b < sum(PARTS[p]):
                block = sum_ref[128 * b:128 * b + 128, :]
                g_ref[128 * i:128 * i + 128, 128 * j:128 * j + 128] = block
                if p == 0 and i != j:
                    g_ref[128 * j:128 * j + 128, 128 * i:128 * i + 128] = block.T

    def all_left(p):
        start, half, piece, hs = sizes(p)
        arrived(from_core.at[pl.ds(hs, half)], sum_send.at[p, 0])
        arrived(from_plane.at[pl.ds(1, 15), pl.ds(hs // 16, piece)], sum_send.at[p, 1])
        arrived(column.at[pl.ds(0, 7), pl.ds(hs // 16, piece)], sum_send.at[p, 2])
        arrived(sum_ref.at[pl.ds(start, 15 * piece)], sum_send.at[p, 3])
        arrived(sum_ref.at[pl.ds(start, half)], sum_send.at[p, 4])

    swap(0)
    swap(1)
    after_swap(0)
    after_spread(0)
    after_swap(1)
    after_ring(0)
    after_spread(1)
    after_back(0)
    after_last(0)

    def between(step):
        for k, go_on in enumerate((after_ring, after_back)):
            @pl.when(step == k)
            def _():
                go_on(1)

    f0, f1 = level([g_ref.at[0:256, 0:256], g_ref.at[256:512, 256:512]], x_ref, between)
    g1_ref[0:128, 0:128] = dot(f0, dot(g_ref[0:256, 0:256], f0, 1, 0), 0, 0)
    g1_ref[128:256, 128:256] = dot(f1, dot(g_ref[256:512, 256:512], f1, 1, 0), 0, 0)
    after_last(1)
    cross = dot(f0, dot(g_ref[0:256, 256:512], f1, 1, 0), 0, 0)
    g1_ref[0:128, 128:256] = cross
    g1_ref[128:256, 0:128] = cross.T
    f, = level([g1_ref], x_ref)
    weights = jnp.concatenate([dot(f[0:128].astype(BF16), f0.astype(BF16), 0, 1, None),
                               dot(f[128:256].astype(BF16), f1.astype(BF16), 0, 1, None)], axis=1).astype(BF16)
    squares = dot(f, dot(g1_ref[...], f, 1, 0), 0, 0)
    diagonal = lax.broadcasted_iota(jnp.int32, (128, 128), 0) == lax.broadcasted_iota(jnp.int32, (128, 128), 1)
    squares = jnp.where(diagonal, squares, 0.0)
    inverse = 1.0 / jnp.sqrt(jnp.sum(squares, axis=1, keepdims=True) + EPSILON)
    energies = jnp.sqrt(jnp.sum(squares, axis=0, keepdims=True) + EPSILON)
    share = jnp.zeros((1, 32), F32)
    for j in range(4):
        share = jnp.where(y == j, energies[:, 32 * j:32 * j + 32], share)
    energy_ref[...] = share

    for c in range(CHUNKS):
        block = jnp.concatenate([rows_ref[c, j] for j in range(4)], axis=1)
        part = (dot(weights, block, 1, 1, None) * inverse).astype(BF16)
        for j in range(4):
            sent_ref[c, j] = part[32 * j:32 * j + 32, :]
        for k in (2, 1, 3):
            py = lax.rem(y + k, 4)
            remote(sent_ref.at[c, py], got_ref.at[c, y], out_send, out_recv.at[c], device(core, x, py, z)).start()
    for c in range(CHUNKS):
        basis_ref[:, at(y * R + c * n, n, 128)] = sent_ref[c, y].astype(F32)
    for c in range(CHUNKS):
        arrived(got_ref.at[c, pl.ds(0, 3)], out_recv.at[c])
        for k in (1, 2, 3):
            py = lax.rem(y + k, 4)
            basis_ref[:, at(py * R + c * n, n, 128)] = got_ref[c, py].astype(F32)
    arrived(rows_ref.at[pl.ds(0, 3)], row_send)
    for p in range(len(PARTS)):
        all_left(p)
    arrived(got_ref.at[pl.ds(0, 3)], out_send)


def body(snapshots):
    R = snapshots.shape[0] // 4
    total = sum(length for _, length in PARTS)
    basis, energies = pl.pallas_call(
        kernel,
        out_shape=(jax.ShapeDtypeStruct((32, 4 * R), F32), jax.ShapeDtypeStruct((1, 32), F32)),
        in_specs=[pl.BlockSpec(memory_space=pl.ANY)],
        out_specs=(pl.BlockSpec(memory_space=pltpu.VMEM),) * 2,
        scratch_shapes=[
            pltpu.VMEM((CHUNKS, 4, R // CHUNKS, 128), BF16),
            pltpu.VMEM((total, 128), F32),
            pltpu.VMEM((total, 128), F32),
            pltpu.VMEM((total // 2, 128), F32),
            pltpu.VMEM((total // 2, 128), F32),
            pltpu.VMEM((16, total // 32, 128), F32),
            pltpu.VMEM((8, total // 32, 128), F32),
            pltpu.VMEM((512, 512), F32),
            pltpu.VMEM((256, 256), F32),
            pltpu.VMEM((2, 256, 128), F32),
            pltpu.VMEM((CHUNKS, 4, 32, R // CHUNKS), BF16),
            pltpu.VMEM((CHUNKS, 4, 32, R // CHUNKS), BF16),
            pltpu.SemaphoreType.DMA,
            pltpu.SemaphoreType.DMA,
            pltpu.SemaphoreType.DMA((CHUNKS,)),
            pltpu.SemaphoreType.DMA((2, 5)),
            pltpu.SemaphoreType.DMA((2, 5)),
            pltpu.SemaphoreType.DMA,
            pltpu.SemaphoreType.DMA((CHUNKS,)),
        ],
        compiler_params=pltpu.CompilerParams(collective_id=0, has_side_effects=True, vmem_limit_bytes=103 * 512 * 1024),
    )(snapshots)
    return basis.T, energies.reshape(32)


def solution(mesh):
    return jax.shard_map(body, mesh=mesh, in_specs=(P("wide", "narrow"),), out_specs=(P("wide", "narrow"), P("narrow")),
                         check_vma=False)
```

time: 102 us -> 94.2 us (0.924)
  Pallas kernels: 98 us -> 92 us
  local copies, waits for them, and re-layouts: 2.78 us -> 1.48 us
    pallas_call x1, Pallas kernels: 98 us -> 92 us  [body(): pl.pallas_call(kernel, out_shape=(jax.ShapeDtypeStruct((32, 4 * R), F32),...]
    unnamed x4 -> x2, local copies, waits for them, and re-layouts: 2.78 us -> 1.48 us
where the time goes in v3:
time: 94.2 us
  Pallas kernels  92 us (98%)
  local copies, waits for them, and re-layouts  1.48 us (2%)
    pallas_call x1, Pallas kernels, body(): pl.pallas_call(kernel, out_shape=(jax.ShapeDtypeStruct((32, 4 * R), F32),...  92 us

profile of v3, /device:TPU:1, one launch (start us, length us, event | category | flops | bytes accessed | tf_op | source)
XLA Modules:
  0.0 94.2 jit_solution(18328971863726037717)
XLA Ops:
  0.6 92.0 %shard_map.30 = (f32[32,8192]{1,0:T(8,128)S(1)}, f32[1,32]{1,0:T(1,128)S(1)}) custom-call(bf16[8192,128]{1,0:T(8,128)(2,1)} %s_ref.1), custom_call_target="tpu_custom_call" | custom-call | tf_op jit(solution)/shard_map/pallas_call | solution.py:294
  92.7 1.0 %copy.5 = f32[8192,32]{0,1:T(8,128)} copy(f32[8192,32]{0,1:T(8,128)S(1)} %bitcast.2) | data formatting | bytes 2097152
  93.7 0.5 copy.6

commit v4 on v3

--- a/solution.py
+++ b/solution.py
@@ -110,27 +110,25 @@
     pltpu.make_async_copy(like, like, sem).wait()
 
 
-def level(grams, y_ref, between=None):
-    for m, g in enumerate(grams):
-        y_ref[m] = (g[:, 0:128] + g[:, 128:256]) * F32(0.5 ** 0.5)
+def level(gram, y_ref, between=None):
+    y_ref[...] = (gram[:, 0:128] + gram[:, 128:256]) * F32(0.5 ** 0.5)
 
     def sweep(step, carry):
-        ys = [y_ref[m] for m in range(len(grams))]
-        linv = inverse_cholesky([dot(v, v, 0, 0) for v in ys])
-        ahead = [jnp.where(step == SWEEPS - 1, v, dot(g[...], v, 1, 0)) for g, v in zip(grams, ys)]
-        for m, v in enumerate(ahead):
-            y_ref[m] = dot(v, linv[m], 1, 1)
+        tall = y_ref[...]
+        linv, = inverse_cholesky([dot(tall, tall, 0, 0)])
+        ahead = jnp.where(step == SWEEPS - 1, tall, dot(gram[...], tall, 1, 0))
+        y_ref[...] = dot(ahead, linv, 1, 1)
         if between is not None:
             between(step)
         return carry
 
     lax.fori_loop(0, SWEEPS, sweep, 0)
-    return [y_ref[m].astype(BF16).astype(F32) for m in range(len(grams))]
+    return y_ref[...].astype(BF16)
 
 
 def kernel(s_ref, basis_ref, energy_ref, rows_ref, part_ref, sum_ref, from_core, halves, from_plane, column,
-           g_ref, g1_ref, x_ref, sent_ref, got_ref,
-           own_sem, row_send, row_recv, sum_send, sum_recv, out_send, out_recv):
+           g_ref, g1_ref, y_ref, f_ref, d_ref, sent_ref, got_ref,
+           own_sem, row_send, row_recv, sum_send, sum_recv, pair_send, pair_recv, out_send, out_recv):
     w = lax.axis_index("wide")
     y = lax.axis_index("narrow")
     core, x, z = lax.rem(w, 2), lax.rem(lax.div(w, 2), 4), lax.div(w, 8)
@@ -210,18 +208,15 @@
     def after_back(p):
         start, half, piece, hs = sizes(p)
         arrived(sum_ref.at[pl.ds(start, 15 * piece)], sum_recv.at[p, 3])
+
+    def last(p):
+        start, half, piece, hs = sizes(p)
         mine = sum_ref.at[at(start + core * half, half)]
         remote(mine, mine, sum_send.at[p, 4], sum_recv.at[p, 4], sibling).start()
 
     def after_last(p):
         start, half, piece, hs = sizes(p)
         arrived(sum_ref.at[pl.ds(start, half)], sum_recv.at[p, 4])
-        for b, (i, j) in enumerate(BLOCKS):
-            if PARTS[p][0] <= 128 * b < sum(PARTS[p]):
-                block = sum_ref[128 * b:128 * b + 128, :]
-                g_ref[128 * i:128 * i + 128, 128 * j:128 * j + 128] = block
-                if p == 0 and i != j:
-                    g_ref[128 * j:128 * j + 128, 128 * i:128 * i + 128] = block.T
 
     def all_left(p):
         start, half, piece, hs = sizes(p)
@@ -229,7 +224,8 @@
         arrived(from_plane.at[pl.ds(1, 15), pl.ds(hs // 16, piece)], sum_send.at[p, 1])
         arrived(column.at[pl.ds(0, 7), pl.ds(hs // 16, piece)], sum_send.at[p, 2])
         arrived(sum_ref.at[pl.ds(start, 15 * piece)], sum_send.at[p, 3])
-        arrived(sum_ref.at[pl.ds(start, half)], sum_send.at[p, 4])
+        if p == 1:
+            arrived(sum_ref.at[pl.ds(start, half)], sum_send.at[p, 4])
 
     swap(0)
     swap(1)
@@ -239,25 +235,46 @@
     after_ring(0)
     after_spread(1)
     after_back(0)
-    after_last(0)
 
     def between(step):
-        for k, go_on in enumerate((after_ring, after_back)):
-            @pl.when(step == k)
-            def _():
-                go_on(1)
-
-    f0, f1 = level([g_ref.at[0:256, 0:256], g_ref.at[256:512, 256:512]], x_ref, between)
-    g1_ref[0:128, 0:128] = dot(f0, dot(g_ref[0:256, 0:256], f0, 1, 0), 0, 0)
-    g1_ref[128:256, 128:256] = dot(f1, dot(g_ref[256:512, 256:512], f1, 1, 0), 0, 0)
+        @pl.when(step == 0)
+        def _():
+            after_ring(1)
+
+        @pl.when(step == 1)
+        def _():
+            after_back(1)
+            last(1)
+
+    low, cross, high = [sum_ref[at(core * 384 + 128 * k, 128), :] for k in range(3)]
+    g_ref[0:128, 0:128] = low
+    g_ref[0:128, 128:256] = cross
+    g_ref[128:256, 0:128] = cross.T
+    g_ref[128:256, 128:256] = high
+    own_factor = level(g_ref, y_ref, between)
+    f_ref[core] = own_factor
+    mine = f_ref.at[core]
+    remote(mine, mine, pair_send.at[0], pair_recv.at[0], sibling).start()
+    wide = own_factor.astype(F32)
+    d_ref[core] = dot(wide, dot(g_ref[...], wide, 1, 0), 0, 0)
+    block = d_ref.at[core]
+    remote(block, block, pair_send.at[1], pair_recv.at[1], sibling).start()
     after_last(1)
-    cross = dot(f0, dot(g_ref[0:256, 256:512], f1, 1, 0), 0, 0)
+    between_pairs = jnp.concatenate(
+        [jnp.concatenate([sum_ref[768 + 256 * i + 128 * j:896 + 256 * i + 128 * j, :] for j in range(2)], axis=1)
+         for i in range(2)], axis=0)
+    arrived(f_ref.at[0], pair_recv.at[0])
+    f0, f1 = f_ref[0], f_ref[1]
+    cross = dot(f0.astype(F32), dot(between_pairs, f1.astype(F32), 1, 0), 0, 0)
+    arrived(d_ref.at[0], pair_recv.at[1])
+    g1_ref[0:128, 0:128] = d_ref[0]
     g1_ref[0:128, 128:256] = cross
     g1_ref[128:256, 0:128] = cross.T
-    f, = level([g1_ref], x_ref)
-    weights = jnp.concatenate([dot(f[0:128].astype(BF16), f0.astype(BF16), 0, 1, None),
-                               dot(f[128:256].astype(BF16), f1.astype(BF16), 0, 1, None)], axis=1).astype(BF16)
-    squares = dot(f, dot(g1_ref[...], f, 1, 0), 0, 0)
+    g1_ref[128:256, 128:256] = d_ref[1]
+    f = level(g1_ref, y_ref)
+    weights = jnp.concatenate([dot(f[0:128], f0, 0, 1, None), dot(f[128:256], f1, 0, 1, None)], axis=1).astype(BF16)
+    wide = f.astype(F32)
+    squares = dot(wide, dot(g1_ref[...], wide, 1, 0), 0, 0)
     diagonal = lax.broadcasted_iota(jnp.int32, (128, 128), 0) == lax.broadcasted_iota(jnp.int32, (128, 128), 1)
     squares = jnp.where(diagonal, squares, 0.0)
     inverse = 1.0 / jnp.sqrt(jnp.sum(squares, axis=1, keepdims=True) + EPSILON)
@@ -285,6 +302,8 @@
     arrived(rows_ref.at[pl.ds(0, 3)], row_send)
     for p in range(len(PARTS)):
         all_left(p)
+    arrived(f_ref.at[0], pair_send.at[0])
+    arrived(d_ref.at[0], pair_send.at[1])
     arrived(got_ref.at[pl.ds(0, 3)], out_send)
 
 
@@ -304,9 +323,11 @@
             pltpu.VMEM((total // 2, 128), F32),
             pltpu.VMEM((16, total // 32, 128), F32),
             pltpu.VMEM((8, total // 32, 128), F32),
-            pltpu.VMEM((512, 512), F32),
             pltpu.VMEM((256, 256), F32),
-            pltpu.VMEM((2, 256, 128), F32),
+            pltpu.VMEM((256, 256), F32),
+            pltpu.VMEM((256, 128), F32),
+            pltpu.VMEM((2, 256, 128), BF16),
+            pltpu.VMEM((2, 128, 128), F32),
             pltpu.VMEM((CHUNKS, 4, 32, R // CHUNKS), BF16),
             pltpu.VMEM((CHUNKS, 4, 32, R // CHUNKS), BF16),
             pltpu.SemaphoreType.DMA,
@@ -314,6 +335,8 @@
             pltpu.SemaphoreType.DMA((CHUNKS,)),
             pltpu.SemaphoreType.DMA((2, 5)),
             pltpu.SemaphoreType.DMA((2, 5)),
+            pltpu.SemaphoreType.DMA((2,)),
+            pltpu.SemaphoreType.DMA((2,)),
             pltpu.SemaphoreType.DMA,
             pltpu.SemaphoreType.DMA((CHUNKS,)),
         ],

time: 94.2 us -> 90.8 us (0.964)
  Pallas kernels: 92 us -> 88.6 us
    pallas_call x1, Pallas kernels: 92 us -> 88.6 us  [body(): pl.pallas_call(kernel, out_shape=(jax.ShapeDtypeStruct((32, 4 * R), F32),...]
where the time goes in v4:
time: 90.8 us; the launch traced here: 90.7 us
  Pallas kernels  88.6 us (98%)
  local copies, waits for them, and re-layouts  1.48 us (2%)
    pallas_call x1, Pallas kernels, body(): pl.pallas_call(kernel, out_shape=(jax.ShapeDtypeStruct((32, 4 * R), F32),...  88.6 us

profile of v4, /device:TPU:1, one launch (start us, length us, event | category | flops | bytes accessed | tf_op | source)
XLA Modules:
  0.0 90.7 jit_solution(8790798107375794424)
XLA Ops:
  0.6 88.6 %shard_map.30 = (f32[32,8192]{1,0:T(8,128)S(1)}, f32[1,32]{1,0:T(1,128)S(1)}) custom-call(bf16[8192,128]{1,0:T(8,128)(2,1)} %s_ref.1), custom_call_target="tpu_custom_call" | custom-call | tf_op jit(solution)/shard_map/pallas_call | solution.py:313
  89.2 1.0 %copy.5 = f32[8192,32]{0,1:T(8,128)} copy(f32[8192,32]{0,1:T(8,128)S(1)} %bitcast.2) | data formatting | bytes 2097152
  90.2 0.5 copy.6

commit v5 on v4

--- a/solution.py
+++ b/solution.py
@@ -13,8 +13,9 @@
 BF16 = jnp.bfloat16
 SWEEPS = 3
 EPSILON = 1e-6
-BLOCKS = ((0, 0), (0, 1), (1, 1), (2, 2), (2, 3), (3, 3), (0, 2), (0, 3), (1, 2), (1, 3))
-PARTS = ((0, 768), (768, 512))
+BLOCKS = ((0, 1), (2, 3), (0, 2), (0, 3), (1, 2), (1, 3))
+PARTS = ((0, 256), (256, 512))
+TILES = 8
 CHUNKS = 4
 
 
@@ -127,8 +128,8 @@
 
 
 def kernel(s_ref, basis_ref, energy_ref, rows_ref, part_ref, sum_ref, from_core, halves, from_plane, column,
-           g_ref, g1_ref, y_ref, f_ref, d_ref, sent_ref, got_ref,
-           own_sem, row_send, row_recv, sum_send, sum_recv, pair_send, pair_recv, out_send, out_recv):
+           all_ref, diag_part, diag_core, diag_plane, diag_column, diag_sum, g_ref, g1_ref, y_ref, f_ref, d_ref, sent_ref, got_ref,
+           own_sem, all_sem, diag_send, diag_recv, row_send, row_recv, sum_send, sum_recv, pair_send, pair_recv, out_send, out_recv):
     w = lax.axis_index("wide")
     y = lax.axis_index("narrow")
     core, x, z = lax.rem(w, 2), lax.rem(lax.div(w, 2), 4), lax.div(w, 8)
@@ -154,15 +155,82 @@
             py = lax.rem(y + k, 4)
             remote(s_ref.at[at(py * R + c * n, n, 16)], rows_ref.at[c, y], row_send, row_recv.at[c],
                    device(core, x, py, z)).start()
+    whole = pltpu.make_async_copy(s_ref, all_ref, all_sem)
+    whole.start()
+
+    holds = core == lax.div(y, 2)
+    diag_part[...] = jnp.zeros_like(diag_part)
+    whole.wait()
+
+    def tile(t, carry):
+        value = all_ref[at(t * (4 * R // TILES), 4 * R // TILES, 16), :]
+        diag_part[...] += dot(value, value, 0, 0, None)
+        return carry
+
+    lax.fori_loop(0, TILES, tile, 0)
+
+    @pl.when(jnp.logical_not(holds))
+    def _():
+        remote(diag_part, diag_core, diag_send.at[0], diag_recv.at[0], sibling).start()
+
+    @pl.when(holds)
+    def _():
+        arrived(diag_core, diag_recv.at[0])
+        diag_part[...] += diag_core[...]
+        for d in range(1, 4):
+            px = lax.rem(x + d, 4)
+            remote(diag_part.at[at(px * 32, 32)], diag_plane.at[d], diag_send.at[1], diag_recv.at[1],
+                   device(core, px, y, z)).start()
+        arrived(diag_plane.at[pl.ds(1, 3)], diag_recv.at[1])
+        total = diag_part[at(x * 32, 32), :]
+        for d in range(1, 4):
+            total = total + diag_plane[d]
+        diag_column[z] = total
+        mine = diag_column.at[z]
+        for d, pz in line:
+            remote(mine, mine, diag_send.at[2], diag_recv.at[2], device(core, x, y, pz)).start()
+
+    def diagonal_back():
+        @pl.when(holds)
+        def _():
+            arrived(diag_column.at[pl.ds(0, 7)], diag_recv.at[2])
+            total = diag_column[0]
+            for k in range(1, 8):
+                total = total + diag_column[k]
+            mine = diag_sum.at[at(lax.rem(y, 2) * 128 + x * 32, 32)]
+            mine[...] = total
+            for d, px, py in plane:
+                remote(mine, mine, diag_send.at[3], diag_recv.at[3], device(core, px, py, z)).start()
+
+    def diagonal_there():
+        @pl.when(holds)
+        def _():
+            arrived(diag_sum.at[pl.ds(0, 224)], diag_recv.at[3])
+
+        @pl.when(jnp.logical_not(holds))
+        def _():
+            arrived(diag_sum, diag_recv.at[3])
+
+    def diagonal_left():
+        @pl.when(jnp.logical_not(holds))
+        def _():
+            arrived(diag_core, diag_send.at[0])
+
+        @pl.when(holds)
+        def _():
+            arrived(diag_plane.at[pl.ds(1, 3)], diag_send.at[1])
+            arrived(diag_column.at[pl.ds(0, 7)], diag_send.at[2])
+            arrived(part_ref.at[pl.ds(0, 480)], diag_send.at[3])
+
     arrived(rows_ref.at[0], own_sem)
     for c in range(CHUNKS):
         arrived(rows_ref.at[c, pl.ds(0, 3)], row_recv.at[c])
         blocks = [rows_ref[c, j] for j in range(4)]
-        for i in range(4):
-            part = dot(blocks[i], jnp.concatenate(blocks[i:], axis=1), 0, 0, None)
-            for j in range(i, 4):
+        for i in range(3):
+            part = dot(blocks[i], jnp.concatenate(blocks[i + 1:], axis=1), 0, 0, None)
+            for j in range(i + 1, 4):
                 b = BLOCKS.index((i, j))
-                part_ref[128 * b:128 * b + 128, :] += part[:, 128 * (j - i):128 * (j - i) + 128]
+                part_ref[128 * b:128 * b + 128, :] += part[:, 128 * (j - i - 1):128 * (j - i)]
 
     q = x * 4 + y
 
@@ -231,9 +299,11 @@
     swap(1)
     after_swap(0)
     after_spread(0)
+    diagonal_back()
     after_swap(1)
     after_ring(0)
     after_spread(1)
+    diagonal_there()
     after_back(0)
 
     def between(step):
@@ -246,11 +316,11 @@
             after_back(1)
             last(1)
 
-    low, cross, high = [sum_ref[at(core * 384 + 128 * k, 128), :] for k in range(3)]
-    g_ref[0:128, 0:128] = low
+    cross = sum_ref[at(core * 128, 128), :]
+    g_ref[0:128, 0:128] = diag_sum[0:128, :]
     g_ref[0:128, 128:256] = cross
     g_ref[128:256, 0:128] = cross.T
-    g_ref[128:256, 128:256] = high
+    g_ref[128:256, 128:256] = diag_sum[128:256, :]
     own_factor = level(g_ref, y_ref, between)
     f_ref[core] = own_factor
     mine = f_ref.at[core]
@@ -261,7 +331,7 @@
     remote(block, block, pair_send.at[1], pair_recv.at[1], sibling).start()
     after_last(1)
     between_pairs = jnp.concatenate(
-        [jnp.concatenate([sum_ref[768 + 256 * i + 128 * j:896 + 256 * i + 128 * j, :] for j in range(2)], axis=1)
+        [jnp.concatenate([sum_ref[256 + 256 * i + 128 * j:384 + 256 * i + 128 * j, :] for j in range(2)], axis=1)
          for i in range(2)], axis=0)
     arrived(f_ref.at[0], pair_recv.at[0])
     f0, f1 = f_ref[0], f_ref[1]
@@ -300,6 +370,7 @@
             py = lax.rem(y + k, 4)
             basis_ref[:, at(py * R + c * n, n, 128)] = got_ref[c, py].astype(F32)
     arrived(rows_ref.at[pl.ds(0, 3)], row_send)
+    diagonal_left()
     for p in range(len(PARTS)):
         all_left(p)
     arrived(f_ref.at[0], pair_send.at[0])
@@ -323,6 +394,12 @@
             pltpu.VMEM((total // 2, 128), F32),
             pltpu.VMEM((16, total // 32, 128), F32),
             pltpu.VMEM((8, total // 32, 128), F32),
+            pltpu.VMEM((4 * R, 128), BF16),
+            pltpu.VMEM((128, 128), F32),
+            pltpu.VMEM((128, 128), F32),
+            pltpu.VMEM((4, 32, 128), F32),
+            pltpu.VMEM((8, 32, 128), F32),
+            pltpu.VMEM((256, 128), F32),
             pltpu.VMEM((256, 256), F32),
             pltpu.VMEM((256, 256), F32),
             pltpu.VMEM((256, 128), F32),
@@ -331,6 +408,9 @@
             pltpu.VMEM((CHUNKS, 4, 32, R // CHUNKS), BF16),
             pltpu.VMEM((CHUNKS, 4, 32, R // CHUNKS), BF16),
             pltpu.SemaphoreType.DMA,
+            pltpu.SemaphoreType.DMA,
+            pltpu.SemaphoreType.DMA((4,)),
+            pltpu.SemaphoreType.DMA((4,)),
             pltpu.SemaphoreType.DMA,
             pltpu.SemaphoreType.DMA((CHUNKS,)),
             pltpu.SemaphoreType.DMA((2, 5)),

time: 90.8 us -> 87.5 us (0.964)
  Pallas kernels: 88.6 us -> 85.3 us
    pallas_call x1, Pallas kernels: 88.6 us -> 85.3 us  [body(): pl.pallas_call(kernel, out_shape=(jax.ShapeDtypeStruct((32, 4 * R), F32),...]
where the time goes in v5:
time: 87.5 us; the launch traced here: 87.4 us
  Pallas kernels  85.3 us (97%)
  local copies, waits for them, and re-layouts  1.48 us (2%)
    pallas_call x1, Pallas kernels, body(): pl.pallas_call(kernel, out_shape=(jax.ShapeDtypeStruct((32, 4 * R), F32),...  85.3 us

profile of v5, /device:TPU:1, one launch (start us, length us, event | category | flops | bytes accessed | tf_op | source)
XLA Modules:
  0.0 87.4 jit_solution(3657807957009732734)
XLA Ops:
  0.6 85.3 %shard_map.30 = (f32[32,8192]{1,0:T(8,128)S(1)}, f32[1,32]{1,0:T(1,128)S(1)}) custom-call(bf16[8192,128]{1,0:T(8,128)(2,1)} %s_ref.1), custom_call_target="tpu_custom_call" | custom-call | tf_op jit(solution)/shard_map/pallas_call | solution.py:384
  85.9 1.0 %copy.5 = f32[8192,32]{0,1:T(8,128)} copy(f32[8192,32]{0,1:T(8,128)S(1)} %bitcast.2) | data formatting | bytes 2097152
  86.9 0.5 copy.6

commit v6 on v5

--- a/solution.py
+++ b/solution.py
@@ -89,6 +89,16 @@
     return [jnp.concatenate([jnp.where(lane <= sub + 8 * r, S[m][r] * jnp.sqrt(inverse_pivots[m][r]), 0.0) for r in range(n // 8)], axis=0) for m in M]
 
 
+def right_factor(a, f):
+    return lax.dot_general(jnp.concatenate(thirds(a), axis=1), jnp.concatenate([f, f, f], axis=0),
+                           (((1,), (0,)), ((), ())), preferred_element_type=F32)
+
+
+def left_factor(f, a):
+    return lax.dot_general(jnp.concatenate([f, f, f], axis=0), jnp.concatenate(thirds(a), axis=0),
+                           (((0,), (0,)), ((), ())), preferred_element_type=F32)
+
+
 def device(core, x, y, z):
     return {"wide": (z * 4 + x) * 2 + core, "narrow": y}
 
@@ -222,7 +232,7 @@
             arrived(diag_column.at[pl.ds(0, 7)], diag_send.at[2])
             arrived(part_ref.at[pl.ds(0, 480)], diag_send.at[3])
 
-    arrived(rows_ref.at[0], own_sem)
+    arrived(rows_ref.at[pl.ds(0, CHUNKS // 4)], own_sem)
     for c in range(CHUNKS):
         arrived(rows_ref.at[c, pl.ds(0, 3)], row_recv.at[c])
         blocks = [rows_ref[c, j] for j in range(4)]
@@ -311,11 +321,6 @@
         def _():
             after_ring(1)
 
-        @pl.when(step == 1)
-        def _():
-            after_back(1)
-            last(1)
-
     cross = sum_ref[at(core * 128, 128), :]
     g_ref[0:128, 0:128] = diag_sum[0:128, :]
     g_ref[0:128, 128:256] = cross
@@ -325,8 +330,9 @@
     f_ref[core] = own_factor
     mine = f_ref.at[core]
     remote(mine, mine, pair_send.at[0], pair_recv.at[0], sibling).start()
-    wide = own_factor.astype(F32)
-    d_ref[core] = dot(wide, dot(g_ref[...], wide, 1, 0), 0, 0)
+    after_back(1)
+    last(1)
+    d_ref[core] = left_factor(own_factor, right_factor(g_ref[...], own_factor))
     block = d_ref.at[core]
     remote(block, block, pair_send.at[1], pair_recv.at[1], sibling).start()
     after_last(1)
@@ -335,7 +341,7 @@
          for i in range(2)], axis=0)
     arrived(f_ref.at[0], pair_recv.at[0])
     f0, f1 = f_ref[0], f_ref[1]
-    cross = dot(f0.astype(F32), dot(between_pairs, f1.astype(F32), 1, 0), 0, 0)
+    cross = left_factor(f0, right_factor(between_pairs, f1))
     arrived(d_ref.at[0], pair_recv.at[1])
     g1_ref[0:128, 0:128] = d_ref[0]
     g1_ref[0:128, 128:256] = cross
@@ -343,8 +349,7 @@
     g1_ref[128:256, 128:256] = d_ref[1]
     f = level(g1_ref, y_ref)
     weights = jnp.concatenate([dot(f[0:128], f0, 0, 1, None), dot(f[128:256], f1, 0, 1, None)], axis=1).astype(BF16)
-    wide = f.astype(F32)
-    squares = dot(wide, dot(g1_ref[...], wide, 1, 0), 0, 0)
+    squares = left_factor(f, right_factor(g1_ref[...], f))
     diagonal = lax.broadcasted_iota(jnp.int32, (128, 128), 0) == lax.broadcasted_iota(jnp.int32, (128, 128), 1)
     squares = jnp.where(diagonal, squares, 0.0)
     inverse = 1.0 / jnp.sqrt(jnp.sum(squares, axis=1, keepdims=True) + EPSILON)
@@ -369,13 +374,13 @@
         for k in (1, 2, 3):
             py = lax.rem(y + k, 4)
             basis_ref[:, at(py * R + c * n, n, 128)] = got_ref[c, py].astype(F32)
-    arrived(rows_ref.at[pl.ds(0, 3)], row_send)
+    arrived(rows_ref.at[pl.ds(0, 3 * CHUNKS // 4)], row_send)
     diagonal_left()
     for p in range(len(PARTS)):
         all_left(p)
     arrived(f_ref.at[0], pair_send.at[0])
     arrived(d_ref.at[0], pair_send.at[1])
-    arrived(got_ref.at[pl.ds(0, 3)], out_send)
+    arrived(got_ref.at[pl.ds(0, 3 * CHUNKS // 4)], out_send)
 
 
 def body(snapshots):

time: 87.5 us -> 86.4 us (0.987)
  Pallas kernels: 85.3 us -> 84.2 us
    pallas_call x1, Pallas kernels: 85.3 us -> 84.2 us  [body(): pl.pallas_call(kernel, out_shape=(jax.ShapeDtypeStruct((32, 4 * R), F32),...]
where the time goes in v6:
time: 86.4 us; the launch traced here: 86.3 us
  Pallas kernels  84.2 us (97%)
  local copies, waits for them, and re-layouts  1.48 us (2%)
    pallas_call x1, Pallas kernels, body(): pl.pallas_call(kernel, out_shape=(jax.ShapeDtypeStruct((32, 4 * R), F32),...  84.2 us

profile of v6, /device:TPU:1, one launch (start us, length us, event | category | flops | bytes accessed | tf_op | source)
XLA Modules:
  0.0 86.3 jit_solution(3844585315956710506)
XLA Ops:
  0.6 84.2 %shard_map.30 = (f32[32,8192]{1,0:T(8,128)S(1)}, f32[1,32]{1,0:T(1,128)S(1)}) custom-call(bf16[8192,128]{1,0:T(8,128)(2,1)} %s_ref.1), custom_call_target="tpu_custom_call" | custom-call | tf_op jit(solution)/shard_map/pallas_call | solution.py:389
  84.8 1.0 %copy.5 = f32[8192,32]{0,1:T(8,128)} copy(f32[8192,32]{0,1:T(8,128)S(1)} %bitcast.2) | data formatting | bytes 2097152
  85.8 0.5 copy.6

commit v7 on v6

--- a/solution.py
+++ b/solution.py
@@ -16,7 +16,7 @@
 BLOCKS = ((0, 1), (2, 3), (0, 2), (0, 3), (1, 2), (1, 3))
 PARTS = ((0, 256), (256, 512))
 TILES = 8
-CHUNKS = 4
+CHUNKS = 8
 
 
 def dot(a, b, ca, cb, precision=HI):

time: 86.4 us -> 86 us (level)
  no operation moved by 1% of the time
where the time goes in v7:
time: 86 us; the launch traced here: 85.9 us
  Pallas kernels  83.8 us (97%)
  local copies, waits for them, and re-layouts  1.48 us (2%)
    pallas_call x1, Pallas kernels, body(): pl.pallas_call(kernel, out_shape=(jax.ShapeDtypeStruct((32, 4 * R), F32),...  83.8 us

profile of v7, /device:TPU:1, one launch (start us, length us, event | category | flops | bytes accessed | tf_op | source)
XLA Modules:
  0.0 85.9 jit_solution(2557825368875931017)
XLA Ops:
  0.6 83.8 %shard_map.30 = (f32[32,8192]{1,0:T(8,128)S(1)}, f32[1,32]{1,0:T(1,128)S(1)}) custom-call(bf16[8192,128]{1,0:T(8,128)(2,1)} %s_ref.1), custom_call_target="tpu_custom_call" | custom-call | tf_op jit(solution)/shard_map/pallas_call | solution.py:389
  84.5 1.0 %copy.5 = f32[8192,32]{0,1:T(8,128)} copy(f32[8192,32]{0,1:T(8,128)S(1)} %bitcast.2) | data formatting | bytes 2097152
  85.4 0.5 copy.6
